TPU v7x, 128 devices: a whole 4x4x4 slice. The times are simulated.
128 devices in a mesh: wide: 32 (over x, z, core), narrow: 4 (over y).
Axes of the slice: x: 4, y: 4, z: 4, core: 2. Of those that a mesh axis runs over, the one named last changes fastest.
Arguments:
- tokens: bfloat16 [256, 588, 384], P(('wide', 'narrow')), may hold values from -6 to 6
- item_frames: int32 [256, 3], P(('wide', 'narrow')), may hold values from 0 to 3, as said below
- ln1_gain: bfloat16 [384], P(('wide', 'narrow')), may hold values from 0.25 to 1.75
- ln1_bias: bfloat16 [384], P(('wide', 'narrow')), may hold values from -2 to 2
- qkv_weight: bfloat16 [384, 1152], P(('wide', 'narrow')), may hold values from -0.3125 to 0.3125
- qv_bias: bfloat16 [768], P(('wide', 'narrow')), may hold values from -2 to 2
- out_weight: bfloat16 [384, 384], P(('wide', 'narrow')), may hold values from -1.25 to 1.25
- out_bias: bfloat16 [384], P(('wide', 'narrow')), may hold values from -2 to 2
- ln2_gain: bfloat16 [384], P(('wide', 'narrow')), may hold values from 0.25 to 1.75
- ln2_bias: bfloat16 [384], P(('wide', 'narrow')), may hold values from -2 to 2
- up_weight: bfloat16 [384, 1536], P(('wide', 'narrow')), may hold values from -0.3125 to 0.3125
- up_bias: bfloat16 [1536], P(('wide', 'narrow')), may hold values from -3 to 3
- down_weight: bfloat16 [1536, 384], P(('wide', 'narrow')), may hold values from -0.15625 to 0.15625
- down_bias: bfloat16 [384], P(('wide', 'narrow')), may hold values from -2 to 2
- cotangent: bfloat16 [256, 588, 384], P(('wide', 'narrow')), may hold values from -6 to 6
Outputs:
- output: bfloat16 [256, 588, 384], P(('wide', 'narrow'))
- input_grad: float32 [256, 588, 384], P(('wide', 'narrow'))
- grad_ln1_gain: float32 [384], P(('wide', 'narrow'))
- grad_ln1_bias: float32 [384], P(('wide', 'narrow'))
- grad_qkv_weight: float32 [384, 1152], P(('wide', 'narrow'))
- grad_qv_bias: float32 [768], P(('wide', 'narrow'))
- grad_out_weight: float32 [384, 384], P(('wide', 'narrow'))
- grad_out_bias: float32 [384], P(('wide', 'narrow'))
- grad_ln2_gain: float32 [384], P(('wide', 'narrow'))
- grad_ln2_bias: float32 [384], P(('wide', 'narrow'))
- grad_up_weight: float32 [384, 1536], P(('wide', 'narrow'))
- grad_up_bias: float32 [1536], P(('wide', 'narrow'))
- grad_down_weight: float32 [1536, 384], P(('wide', 'narrow'))
- grad_down_bias: float32 [384], P(('wide', 'narrow'))
Inputs may be any that keep to these rules, and one draw needn't show every extreme that they name: `item_frames`: row s gives the frames of the items packed into slot s, in order; zeros stand only after the last item, a row sums to 3 or less, and the rest of the slot is padding. Every aligned block of 2 slots holds a slot with a single item of 3 frames.
All inputs are finite; a program needn't handle non-finite values.
Results may differ from a plain program's by a relative error of at most 0.015.
Values may be sent and summed in bfloat16 or wider, within the bound.
No kernel may reach another device: no remote copies, remote signals or barrier semaphores. Data moves between devices by JAX's collectives and lax.ppermute only.
A program may use at most 192 MiB of HBM per device.

v0:
```python
import math

import jax
import jax.numpy as jnp
from jax import lax
from jax.sharding import Mesh
from jax.sharding import PartitionSpec as P

HEADS = 16
FRAME = 196
WIDE_NARROW = ("wide_0", "wide_1", "wide_2", "narrow")


EPSILON = 1e-05
NEGATIVE = -1e30


def in_one_piece(arrays, axis, dim, along):
    widths = [math.prod(a.shape[along:]) for a in arrays]
    both = jnp.concatenate(
        [a.reshape(*a.shape[:along], w) for a, w in zip(arrays, widths)], axis=along
    )
    whole = lax.all_gather(both, axis, axis=dim, tiled=True)
    blocks = jnp.split(whole, [sum(widths[:k]) for k in range(1, len(widths))], axis=along)
    return tuple(
        (b.reshape(*whole.shape[:along], *a.shape[along:]) for a, b in zip(arrays, blocks))
    )


def split_up(shard, dim, devices):
    dims = shard.shape
    blocks = shard.reshape(*dims[:dim], devices, dims[dim] // devices, *dims[dim + 1 :])
    return jnp.moveaxis(blocks, dim, 0)


def summed_on_arrival(shard, axis, dim):
    blocks = split_up(shard, dim, lax.axis_size(axis))
    arrived = lax.all_to_all(blocks, axis, split_axis=0, concat_axis=0, tiled=True)
    return arrived.sum(axis=0)


def summed_rows(shard, axes, dim):
    far, near = axes
    own = summed_on_arrival(split_up(shard, dim, lax.axis_size(far)), near, dim + 1)
    return jnp.sum(lax.all_to_all(own, far, 0, 0, tiled=True), axis=0)


def in_one_piece_2(arrays, axis, dim, along):
    widths = [math.prod(a.shape[along:]) for a in arrays]
    both = jnp.concatenate(
        [a.reshape(*a.shape[:along], w) for a, w in zip(arrays, widths)], axis=along
    )
    whole = summed_rows(both, axis, dim)
    blocks = jnp.split(whole, [sum(widths[:k]) for k in range(1, len(widths))], axis=along)
    return tuple(
        (b.reshape(*whole.shape[:along], *a.shape[along:]) for a, b in zip(arrays, blocks))
    )


def product(left, right):
    return jnp.dot(left, right, preferred_element_type=jnp.float32)


def product_left_t(left, right):
    return lax.dot_general(
        left, right, (((0,), (0,)), ((), ())), preferred_element_type=jnp.float32
    )


def product_right_t(left, right):
    return lax.dot_general(
        left, right, (((1,), (1,)), ((), ())), preferred_element_type=jnp.float32
    )


def norm_forward(values, gain, offset):
    average = jnp.mean(values, axis=-1, keepdims=True)
    centred = values - average
    variance = jnp.mean(centred * centred, axis=-1, keepdims=True)
    inverse = lax.rsqrt(variance + EPSILON)
    normed = centred * inverse
    return (normed * gain + offset, normed, inverse)


def norm_backward(grad_out, normed, inverse, gain):
    scaled = grad_out * gain
    mean_one = jnp.mean(scaled, axis=-1, keepdims=True)
    mean_two = jnp.mean(scaled * normed, axis=-1, keepdims=True)
    grad_in = inverse * (scaled - mean_one - normed * mean_two)
    return (grad_in, jnp.sum(grad_out * normed, axis=0), jnp.sum(grad_out, axis=0))


def slot_visible(counts, slot_span):
    frame_of = jnp.arange(slot_span, dtype=jnp.int32) // FRAME
    first_end = counts[0]
    second_end = first_end + counts[1]
    third_end = second_end + counts[2]
    group_of = (
        (frame_of >= first_end).astype(jnp.int32)
        + (frame_of >= second_end).astype(jnp.int32)
        + (frame_of >= third_end).astype(jnp.int32)
    )
    return (group_of[:, None] == group_of[None, :]) & (frame_of[None, :] <= frame_of[:, None])


def masked_scores(query_heads, key_heads, visible, score_scale):
    raw_scores = (
        jnp.einsum("qhd,khd->hqk", query_heads, key_heads, preferred_element_type=jnp.float32)
        * score_scale
    )
    return jnp.where(visible[None], raw_scores, NEGATIVE)


def shards(
    tokens,
    item_frames,
    ln1_gain,
    ln1_bias,
    qkv_weight,
    qv_bias,
    out_weight,
    out_bias,
    ln2_gain,
    ln2_bias,
    up_weight,
    up_bias,
    down_weight,
    down_bias,
    cotangent,
):
    slot_count, slot_span, model_width = tokens.shape
    row_count = slot_count * slot_span
    head_count = HEADS
    head_size = model_width // head_count
    score_scale = 1.0 / jnp.sqrt(jnp.float32(head_size))
    forward_params = (
        lax.all_gather(ln1_gain, WIDE_NARROW, axis=0, tiled=True),
        *in_one_piece((ln1_bias, qkv_weight), WIDE_NARROW, 0, 1),
        lax.all_gather(qv_bias, WIDE_NARROW, axis=0, tiled=True),
        *in_one_piece((out_weight, out_bias, ln2_gain, ln2_bias, up_weight), WIDE_NARROW, 0, 1),
        *in_one_piece((up_bias, down_weight), WIDE_NARROW, 0, 1),
        lax.all_gather(down_bias, WIDE_NARROW, axis=0, tiled=True),
    )
    (
        gain_one,
        bias_one,
        qkv_full,
        qv_full,
        out_full,
        out_b,
        gain_two,
        bias_two,
        up_full,
        up_b,
        down_full,
        down_b,
    ) = forward_params
    inputs = tokens.astype(jnp.float32).reshape(row_count, model_width)
    first, normed_one, inverse_one = norm_forward(
        inputs, gain_one.astype(jnp.float32), bias_one.astype(jnp.float32)
    )
    first_low = first.astype(jnp.bfloat16)
    projected = product(first_low, qkv_full)
    qv_float = qv_full.astype(jnp.float32)
    query_low = (projected[:, :model_width] + qv_float[:model_width]).astype(jnp.bfloat16)
    key_low = projected[:, model_width : 2 * model_width].astype(jnp.bfloat16)
    value_low = (projected[:, 2 * model_width :] + qv_float[model_width:]).astype(jnp.bfloat16)
    query_heads = query_low.reshape(slot_count, slot_span, head_count, head_size)
    key_heads = key_low.reshape(slot_count, slot_span, head_count, head_size)
    value_heads = value_low.reshape(slot_count, slot_span, head_count, head_size)

    def attend_forward(data):
        slot_query, slot_key, slot_value, counts = data
        visible = slot_visible(counts, slot_span)
        masked = masked_scores(slot_query, slot_key, visible, score_scale)
        row_peak = jnp.max(masked, axis=-1, keepdims=True)
        weights = jnp.exp(masked - row_peak)
        row_total = jnp.sum(weights, axis=-1, keepdims=True)
        probs_low = (weights / row_total).astype(jnp.bfloat16)
        slot_mixed = jnp.einsum(
            "hqk,khd->qhd", probs_low, slot_value, preferred_element_type=jnp.float32
        )
        return (slot_mixed.astype(jnp.bfloat16), row_peak + jnp.log(row_total))

    mixed_heads, log_total = lax.map(
        attend_forward, (query_heads, key_heads, value_heads, item_frames)
    )
    mixed_low = mixed_heads.reshape(row_count, model_width)
    resid = inputs + product(mixed_low, out_full) + out_b.astype(jnp.float32)
    second, normed_two, inverse_two = norm_forward(
        resid, gain_two.astype(jnp.float32), bias_two.astype(jnp.float32)
    )
    second_low = second.astype(jnp.bfloat16)
    up_pre = product(second_low, up_full) + up_b.astype(jnp.float32)
    activated, gelu_pull = jax.vjp(jax.nn.gelu, up_pre)
    activated_low = activated.astype(jnp.bfloat16)
    result = resid + product(activated_low, down_full) + down_b.astype(jnp.float32)
    output = result.astype(jnp.bfloat16).reshape(slot_count, slot_span, model_width)
    (
        back_gain_one,
        unused_one,
        back_qkv,
        unused_two,
        back_out,
        unused_three,
        back_gain_two,
        unused_four,
        back_up,
        unused_five,
        back_down,
        unused_six,
    ) = forward_params
    grad_result = cotangent.astype(jnp.float32).reshape(row_count, model_width)
    grad_branch = cotangent.reshape(row_count, model_width)
    grad_down_weight = product_left_t(activated_low, grad_branch)
    grad_down_bias = jnp.sum(grad_branch.astype(jnp.float32), axis=0)
    grad_activated = product_right_t(grad_branch, back_down)
    grad_up = gelu_pull(grad_activated)[0].astype(jnp.bfloat16)
    grad_up_weight = product_left_t(second_low, grad_up)
    grad_up_bias = jnp.sum(grad_up.astype(jnp.float32), axis=0)
    grad_second = product_right_t(grad_up, back_up)
    grad_resid_norm, grad_gain_two, grad_bias_two = norm_backward(
        grad_second, normed_two, inverse_two, back_gain_two.astype(jnp.float32)
    )
    grad_resid = grad_result + grad_resid_norm
    grad_attended = grad_resid.astype(jnp.bfloat16)
    grad_out_weight = product_left_t(mixed_low, grad_attended)
    grad_out_bias = jnp.sum(grad_attended.astype(jnp.float32), axis=0)
    grad_mixed = product_right_t(grad_attended, back_out).astype(jnp.bfloat16)
    grad_mixed_heads = grad_mixed.reshape(slot_count, slot_span, head_count, head_size)

    def attend_backward(data):
        slot_query, slot_key, slot_value, slot_grad, slot_log, counts = data
        visible = slot_visible(counts, slot_span)
        again = masked_scores(slot_query, slot_key, visible, score_scale)
        probs = jnp.exp(again - slot_log)
        probs_again = probs.astype(jnp.bfloat16)
        grad_probs = jnp.einsum(
            "qhd,khd->hqk", slot_grad, slot_value, preferred_element_type=jnp.float32
        )
        row_dot = jnp.sum(probs * grad_probs, axis=-1, keepdims=True)
        grad_scores = (probs * (grad_probs - row_dot)).astype(jnp.bfloat16)
        slot_gq = (
            jnp.einsum("hqk,khd->qhd", grad_scores, slot_key, preferred_element_type=jnp.float32)
            * score_scale
        )
        slot_gk = (
            jnp.einsum("hqk,qhd->khd", grad_scores, slot_query, preferred_element_type=jnp.float32)
            * score_scale
        )
        slot_gv = jnp.einsum(
            "hqk,qhd->khd", probs_again, slot_grad, preferred_element_type=jnp.float32
        )
        return (
            slot_gq.astype(jnp.bfloat16),
            slot_gk.astype(jnp.bfloat16),
            slot_gv.astype(jnp.bfloat16),
        )

    grad_q_heads, grad_k_heads, grad_v_heads = lax.map(
        attend_backward,
        (query_heads, key_heads, value_heads, grad_mixed_heads, log_total, item_frames),
    )
    grad_queries_low = grad_q_heads.reshape(row_count, model_width)
    grad_keys_low = grad_k_heads.reshape(row_count, model_width)
    grad_values_low = grad_v_heads.reshape(row_count, model_width)
    grad_projected = jnp.concatenate([grad_queries_low, grad_keys_low, grad_values_low], axis=1)
    grad_qkv_weight = product_left_t(first_low, grad_projected)
    grad_qv_bias = jnp.concatenate(
        [
            jnp.sum(grad_queries_low.astype(jnp.float32), axis=0),
            jnp.sum(grad_values_low.astype(jnp.float32), axis=0),
        ]
    )
    grad_first = product_right_t(grad_projected, back_qkv)
    grad_inputs_norm, grad_gain_one, grad_bias_one = norm_backward(
        grad_first, normed_one, inverse_one, back_gain_one.astype(jnp.float32)
    )
    input_grad = (grad_resid + grad_inputs_norm).reshape(slot_count, slot_span, model_width)
    summed = (
        summed_rows(grad_gain_one, (("wide_0", "wide_1"), ("wide_2", "narrow")), 0),
        *in_one_piece_2(
            (grad_bias_one, grad_qkv_weight), (("wide_0", "wide_1"), ("wide_2", "narrow")), 0, 1
        ),
        summed_rows(grad_qv_bias, (("wide_0", "wide_1"), ("wide_2", "narrow")), 0),
        *in_one_piece_2(
            (grad_out_weight, grad_out_bias, grad_gain_two, grad_bias_two, grad_up_weight),
            (("wide_0", "wide_1"), ("wide_2", "narrow")),
            0,
            1,
        ),
        *in_one_piece_2(
            (grad_up_bias, grad_down_weight), (("wide_0", "wide_1"), ("wide_2", "narrow")), 0, 1
        ),
        summed_rows(grad_down_bias, (("wide_0", "wide_1"), ("wide_2", "narrow")), 0),
    )
    return (
        output,
        input_grad,
        summed[0],
        summed[1],
        summed[2],
        summed[3],
        summed[4],
        summed[5],
        summed[6],
        summed[7],
        summed[8],
        summed[9],
        summed[10],
        summed[11],
    )


def solution(mesh):
    split = Mesh(
        mesh.devices.reshape(4, 4, 2, mesh.shape["narrow"]),
        ("wide_0", "wide_1", "wide_2", "narrow"),
    )
    return jax.shard_map(
        shards,
        mesh=split,
        in_specs=(
            P(WIDE_NARROW, None, None),
            P(WIDE_NARROW, None),
            P(WIDE_NARROW),
            P(WIDE_NARROW),
            P(WIDE_NARROW, None),
            P(WIDE_NARROW),
            P(WIDE_NARROW, None),
            P(WIDE_NARROW),
            P(WIDE_NARROW),
            P(WIDE_NARROW),
            P(WIDE_NARROW, None),
            P(WIDE_NARROW),
            P(WIDE_NARROW, None),
            P(WIDE_NARROW),
            P(WIDE_NARROW, None, None),
        ),
        out_specs=(
            P(WIDE_NARROW, None, None),
            P(WIDE_NARROW, None, None),
            P(WIDE_NARROW),
            P(WIDE_NARROW),
            P(WIDE_NARROW, None),
            P(WIDE_NARROW),
            P(WIDE_NARROW, None),
            P(WIDE_NARROW),
            P(WIDE_NARROW),
            P(WIDE_NARROW),
            P(WIDE_NARROW, None),
            P(WIDE_NARROW),
            P(WIDE_NARROW, None),
            P(WIDE_NARROW),
        ),
        check_vma=False,
    )
```

profile of v0, /device:TPU:2, one launch (start us, length us, event | category | flops | bytes accessed | tf_op | source)
XLA Modules:
  0.0 714.8 jit_solution(15208515102629127312)
XLA Ops:
  28.0 67.7 %all-reduce.3 = (bf16[768]{0:T(1024)(128)(2,1)S(1)}, bf16[384]{0:T(512)(128)(2,1)S(1)}, bf16[384]{0:T(512)(128)(2,1)}) all-reduce(bf16[768]{0:T(1024)(128)(2,1)S(1)} %dynamic-update-slice.1, bf16[384]{0:T(512)(128)(2,1)S(1)} %dynamic-update-slice, ...), channel_id=1, replica_groups=mesh['wide_0'=4,'wide_1'=4,'wide_2'=2,'narrow'=4] {'wide_0','wide_1','wi..., use_global_device_ids=true, to_apply=%add.1 | all-reduce | flops 1536 | bytes 6144
  96.2 62.5 %all-gather = bf16[128,3,1153]{2,1,0:T(4,128)(2,1)S(1)} all-gather(bf16[1,3,1153]{2,1,0:T(4,128)(2,1)S(1)} %maximum_bitcast_fusion.4), channel_id=1, replica_groups=mesh['wide_0'=4,'wide_1'=4,'wide_2'=2,'narrow'=4] {'wide_0','wide_1','wi..., dimensions={0}, use_global_device_ids=true | all-gather | bytes 892422 | tf_op jit(solution)/shard_map/all_gather | solution.py:23
  184.2 68.9 %while.30 = (s32[]{:T(128)}, bf16[2,588,16,24]{1,3,2,0:T(8,128)(2,1)}, f32[2,16,588,1]{2,1,3,0:T(8,128)S(1)}, bf16[2,588,16,24]{1,3,2,0:T(8,128)(2,1)}, s32[2,3]...) while((s32[]{:T(128)}, ...), condition=%wide.region_5.6_spmd, body=%wide.region_2.5_spmd.sunk | while | flops 598708672 | bytes 160718912 | solution.py:185
  192.6 8.0 %copy-done = f32[16,588,588]{1,2,0:T(8,128)} copy-done((f32[16,588,588]{1,2,0:T(8,128)}, f32[16,588,588]{1,2,0:T(8,128)S(1)}, u32[]{:S(2)}) %copy-start) | copy-done | bytes 22127640 | tf_op jit(solution)/shard_map/while
  200.6 6.1 fusion.148
  206.7 12.1 %fusion.149 = bf16[2,588,16,24]{1,3,2,0:T(8,128)(2,1)} fusion(bf16[2,588,16,24]{1,3,2,0:T(8,128)(2,1)} %get-tuple-element.708, s32[]{:T(128)S(6)} %copy.505, f32[16,588,588]{1,2,0:T(8,128)} %copy-done, f32[16,588]{1,0:T(8,128)S(1)} %fusion.148, f32[16,588]{1,0:T(8,128)S(1)} %get-tuple-element.681, pred[588,588]{0,1:T(8,128)(4,1)S(1)} %compare_and_fusion.4, ...), kind=kOutput, calls=%fused_computation.9.clone.1 | convolution fusion | flops 293416704 | bytes 25653392 | tf_op jit(solution)/shard_map/while/body/eval_jaxpr/hqk,khd->qhd/dot_general | solution.py:180
  226.9 8.0 %copy-done = f32[16,588,588]{1,2,0:T(8,128)} copy-done((f32[16,588,588]{1,2,0:T(8,128)}, f32[16,588,588]{1,2,0:T(8,128)S(1)}, u32[]{:S(2)}) %copy-start) | copy-done | bytes 22127640 | tf_op jit(solution)/shard_map/while
  234.9 6.1 fusion.148
  241.0 12.1 %fusion.149 = bf16[2,588,16,24]{1,3,2,0:T(8,128)(2,1)} fusion(bf16[2,588,16,24]{1,3,2,0:T(8,128)(2,1)} %get-tuple-element.708, s32[]{:T(128)S(6)} %copy.505, f32[16,588,588]{1,2,0:T(8,128)} %copy-done, f32[16,588]{1,0:T(8,128)S(1)} %fusion.148, f32[16,588]{1,0:T(8,128)S(1)} %get-tuple-element.681, pred[588,588]{0,1:T(8,128)(4,1)S(1)} %compare_and_fusion.4, ...), kind=kOutput, calls=%fused_computation.9.clone.1 | convolution fusion | flops 293416704 | bytes 25653392 | tf_op jit(solution)/shard_map/while/body/eval_jaxpr/hqk,khd->qhd/dot_general | solution.py:180
  291.9 8.0 %convert_reduce_fusion = (f32[1536]{0:T(1024)}, bf16[1176,1536]{1,0:T(8,128)(2,1)S(1)}) fusion(f32[1176,1536]{1,0:T(8,128)S(1)} %get-tuple-element.562, bf16[1176,384]{1,0:T(8,128)(2,1)S(1)} %copy-done.21, bf16[1536,385]{1,0:T(8,128)(2,1)S(1)} %copy-done.17), kind=kOutput, calls=%fused_computation.102 | convolution fusion | flops 1427003904 | bytes 12926976 | tf_op jit(solution)/shard_map/dot_general | solution.py:71
  318.9 135.6 %while.31 = (s32[]{:T(128)}, bf16[2,588,16,24]{1,3,2,0:T(8,128)(2,1)}, bf16[2,588,16,24]{1,3,2,0:T(8,128)(2,1)}, bf16[2,588,16,24]{1,3,2,0:T(8,128)(2,1)}, bf16[...) while((s32[]{:T(128)}, ...), condition=%wide.region_12.13_spmd, body=%wide.region_10.12_spmd.sunk | while | flops 1412801792 | bytes 186120976 | solution.py:260
  322.9 9.8 %fusion.158 = f32[16,588,588]{1,2,0:T(8,128)} fusion(bf16[2,588,16,24]{1,3,2,0:T(8,128)(2,1)S(1)} %get-tuple-element.751, s32[]{:T(128)S(6)} %copy.515, bf16[2,588,16,24]{1,3,2,0:T(8,128)(2,1)S(1)} %get-tuple-element.749), kind=kOutput, calls=%fused_computation.54.clone.1 | convolution fusion | flops 265531392 | bytes 23111680 | tf_op jit(solution)/shard_map/while/body/eval_jaxpr/qhd,khd->hqk/dot_general | solution.py:108
  332.7 14.3 %fusion.162 = bf16[2,588,16,24]{1,3,2,0:T(8,128)(2,1)} fusion(bf16[2,588,16,24]{1,3,2,0:T(8,128)(2,1)} %get-tuple-element.737, s32[]{:T(128)S(6)} %copy.515, f32[16,588,588]{1,2,0:T(8,128)} %fusion.158, f32[16,588]{1,0:T(8,128)S(1)} %dynamic-slice_bitcast_fusion.2, pred[588,588]{0,1:T(8,128)(4,1)S(1)} %compare_and_fusion.5, ...), kind=kOutput, calls=%fused_computation.48.clone.1 | convolution fusion | flops 287884800 | bytes 25615760 | tf_op jit(solution)/shard_map/while/body/eval_jaxpr/hqk,qhd->khd/dot_general | solution.py:251
  347.0 16.5 %multiply_reduce_fusion.10 = (f32[16,588]{1,0:T(8,128)S(1)}, f32[16,588,588]{1,2,0:T(8,128)}) fusion(f32[16,588,588]{1,2,0:T(8,128)} %fusion.158, f32[16,588]{1,0:T(8,128)S(1)} %dynamic-slice_bitcast_fusion.2, pred[588,588]{0,1:T(8,128)(4,1)S(1)} %compare_and_fusion.5, bf16[2,588,16,24]{1,3,2,0:T(8,128)(2,1)} %get-tuple-element.754, s32[]{:T(128)S(6)} %copy.515, ...), kind=kOutput, calls=%fused_computation.32.clone.1 | convolution fusion | flops 293181504 | bytes 47781008 | tf_op jit(solution)/shard_map/while/body/eval_jaxpr/qhd,khd->hqk/dot_general | solution.py:238
  363.5 16.3 %multiply_convert_fusion.10 = bf16[16,588,588]{1,2,0:T(8,128)(2,1)S(1)} fusion(f32[16,588,588]{1,2,0:T(8,128)} %get-tuple-element.697, f32[16,588,588]{1,2,0:T(8,128)} %fusion.158, f32[16,588]{1,0:T(8,128)S(1)} %get-tuple-element.698, f32[16,588]{1,0:T(8,128)S(1)} %dynamic-slice_bitcast_fusion.2, pred[588,588]{0,1:T(8,128)(4,1)S(1)} %compare_and_fusion.5), kind=kLoop, calls=%fused_computation.31.clone.1 | loop fusion | flops 33191424 | bytes 55740048 | tf_op jit(solution)/shard_map/while/body/eval_jaxpr/convert_element_type | solution.py:242
  390.4 9.8 %fusion.158 = f32[16,588,588]{1,2,0:T(8,128)} fusion(bf16[2,588,16,24]{1,3,2,0:T(8,128)(2,1)S(1)} %get-tuple-element.751, s32[]{:T(128)S(6)} %copy.515, bf16[2,588,16,24]{1,3,2,0:T(8,128)(2,1)S(1)} %get-tuple-element.749), kind=kOutput, calls=%fused_computation.54.clone.1 | convolution fusion | flops 265531392 | bytes 23111680 | tf_op jit(solution)/shard_map/while/body/eval_jaxpr/qhd,khd->hqk/dot_general | solution.py:108
  400.2 14.3 %fusion.162 = bf16[2,588,16,24]{1,3,2,0:T(8,128)(2,1)} fusion(bf16[2,588,16,24]{1,3,2,0:T(8,128)(2,1)} %get-tuple-element.737, s32[]{:T(128)S(6)} %copy.515, f32[16,588,588]{1,2,0:T(8,128)} %fusion.158, f32[16,588]{1,0:T(8,128)S(1)} %dynamic-slice_bitcast_fusion.2, pred[588,588]{0,1:T(8,128)(4,1)S(1)} %compare_and_fusion.5, ...), kind=kOutput, calls=%fused_computation.48.clone.1 | convolution fusion | flops 287884800 | bytes 25615760 | tf_op jit(solution)/shard_map/while/body/eval_jaxpr/hqk,qhd->khd/dot_general | solution.py:251
  414.5 16.5 %multiply_reduce_fusion.10 = (f32[16,588]{1,0:T(8,128)S(1)}, f32[16,588,588]{1,2,0:T(8,128)}) fusion(f32[16,588,588]{1,2,0:T(8,128)} %fusion.158, f32[16,588]{1,0:T(8,128)S(1)} %dynamic-slice_bitcast_fusion.2, pred[588,588]{0,1:T(8,128)(4,1)S(1)} %compare_and_fusion.5, bf16[2,588,16,24]{1,3,2,0:T(8,128)(2,1)} %get-tuple-element.754, s32[]{:T(128)S(6)} %copy.515, ...), kind=kOutput, calls=%fused_computation.32.clone.1 | convolution fusion | flops 293181504 | bytes 47781008 | tf_op jit(solution)/shard_map/while/body/eval_jaxpr/qhd,khd->hqk/dot_general | solution.py:238
  431.0 16.3 %multiply_convert_fusion.10 = bf16[16,588,588]{1,2,0:T(8,128)(2,1)S(1)} fusion(f32[16,588,588]{1,2,0:T(8,128)} %get-tuple-element.697, f32[16,588,588]{1,2,0:T(8,128)} %fusion.158, f32[16,588]{1,0:T(8,128)S(1)} %get-tuple-element.698, f32[16,588]{1,0:T(8,128)S(1)} %dynamic-slice_bitcast_fusion.2, pred[588,588]{0,1:T(8,128)(4,1)S(1)} %compare_and_fusion.5), kind=kLoop, calls=%fused_computation.31.clone.1 | loop fusion | flops 33191424 | bytes 55740048 | tf_op jit(solution)/shard_map/while/body/eval_jaxpr/convert_element_type | solution.py:242
  530.2 6.0 copy.462
  536.2 7.1 dot_general.106
  543.9 10.4 %all-to-all-done.2 = f32[8,16,3,1153]{3,1,2,0:T(8,128)} async-done(((f32[8,16,3,1153]{3,1,2,0:T(8,128)}), f32[8,16,3,1153]{3,1,2,0:T(8,128)}, u32[]{:S(2)}, u32[]{:S(2)}) %all-to-all-start.2) | async-done | bytes 1771040 | tf_op jit(solution)/shard_map/all_to_all | solution.py:38
  559.0 7.0 fusion.99
  569.0 7.3 %all-to-all-start.3 = ((f32[16,3,1153]{2,1,0:T(4,128)}), f32[16,3,1153]{2,1,0:T(4,128)S(1)}, u32[]{:S(2)}, u32[]{:S(2)}) async-start(f32[16,3,1153]{2,1,0:T(4,128)} %copy.450), calls=%async_computation.3 | async-start | bytes 655360 | tf_op jit(solution)/shard_map/all_to_all | solution.py:45
  594.1 5.9 fusion.114
  604.5 8.9 %concatenate.57 = f32[16,8,3,1923]{3,2,1,0:T(4,128)} concatenate(f32[16,8,3,384]{3,2,1,0:T(4,128)S(1)} %copy.456, f32[16,8,3,1]{3,2,1,0:T(4,128)S(1)} %concatenate.60, f32[16,8,3,1]{3,2,1,0:T(4,128)S(1)} %concatenate.61, f32[16,8,3,1]{3,2,1,0:T(4,128)S(1)} %concatenate.62, f32[16,8,3,1536]{3,2,1,0:T(4,128)} %concatenate.56), dimensions={3} | concatenate | bytes 5907456 | tf_op jit(solution)/shard_map/concatenate | solution.py:50
  619.1 7.9 %all-to-all-done.8 = f32[8,16,12,385]{3,1,2,0:T(8,128)} async-done(((f32[8,16,12,385]{3,1,2,0:T(8,128)}), f32[8,16,12,385]{3,1,2,0:T(8,128)}, u32[]{:S(2)}, u32[]{:S(2)}) %all-to-all-start.8) | async-done | bytes 2365472 | tf_op jit(solution)/shard_map/all_to_all | solution.py:38
  632.0 7.5 %fusion.84 = bf16[1176,384]{1,0:T(8,128)(2,1)} fusion(f32[1176,384]{1,0:T(8,128)} %copy-done.4, f32[1176,1536]{1,0:T(8,128)} %copy-done.51, bf16[1536,385]{1,0:T(8,128)(2,1)S(1)} %copy-done.18, f32[384]{0:T(512)S(1)} %convert_element_type.288), kind=kOutput, calls=%fused_computation.110 | convolution fusion | flops 1404877824 | bytes 11116544 | tf_op jit(solution)/shard_map/dot_general | solution.py:61
  642.8 26.4 %all-to-all-done.6 = f32[8,16,3,1923]{3,1,2,0:T(8,128)} async-done(((f32[8,16,3,1923]{3,1,2,0:T(8,128)}), f32[8,16,3,1923]{3,1,2,0:T(8,128)}, u32[]{:S(2)}, u32[]{:S(2)}) %all-to-all-start.6) | async-done | bytes 2953760 | tf_op jit(solution)/shard_map/all_to_all | solution.py:38
  669.2 6.5 all-to-all-start.9
  678.9 6.4 all-to-all-done.9
  685.2 6.1 all-to-all-start.7
  (298 shorter events, 272.9 us)
Async XLA Ops:
  7.2 15.7 %copy-start.10 = (bf16[2,588,384]{2,0,1:T(2,128)(2,1)S(1)}, bf16[2,588,384]{2,0,1:T(2,128)(2,1)}, u32[]{:S(2)}) copy-start(bf16[2,588,384]{2,0,1:T(2,128)(2,1)} %param.19) | copy-start | bytes 2709508
  7.2 264.0 %all-gather.8.cloned.1.call-start = ((), (), s32[]{:S(2)}) async-start(), calls=%async_computation.13 | async-start | bytes 2113536 | tf_op jit(solution)/shard_map/all_gather | solution.py:23
  12.4 257.3 %all-to-all-start.10 = ((f32[8,16,3]{1,2,0:T(4,128)}), f32[8,16,3]{1,2,0:T(4,128)}, u32[]{:S(2)}, u32[]{:S(2)}) async-start(f32[8,16,3]{1,2,0:T(4,128)} %copy.466), calls=%async_computation.10 | async-start | bytes 32768 | tf_op jit(solution)/shard_map/all_to_all | solution.py:38
  16.9 259.3 %all-gather.6.cloned.1.call-start = ((), (), s32[]{:S(2)}) async-start(), calls=%async_computation.12 | async-start | bytes 2113536 | tf_op jit(solution)/shard_map/all_gather | solution.py:23
  22.8 73.4 %copy-start.35 = (bf16[3,1152]{1,0:T(4,128)(2,1)S(1)}, bf16[3,1152]{1,0:T(4,128)(2,1)}, u32[]{:S(2)}) copy-start(bf16[3,1152]{1,0:T(4,128)(2,1)} %param.23) | copy-start | bytes 20740
  95.8 65.9 %copy-start.29 = (f32[384]{0:T(512)}, f32[384]{0:T(512)S(1)}, u32[]{:S(2)}) copy-start(f32[384]{0:T(512)S(1)} %convert_element_type.271) | copy-start | bytes 4612
  96.1 65.6 %copy-start.23 = (f32[1176]{0:T(1024)}, f32[1176]{0:T(1024)S(1)}, u32[]{:S(2)}) copy-start(f32[1176]{0:T(1024)S(1)} %rsqrt.20) | copy-start | bytes 14116
  96.1 65.5 %copy-start.25 = (f32[1176]{0:T(1024)}, f32[1176]{0:T(1024)S(1)}, u32[]{:S(2)}) copy-start(f32[1176]{0:T(1024)S(1)} %div.115) | copy-start | bytes 14116
  177.3 6.9 copy-start.45
  192.6 8.0 %copy-start = (f32[16,588,588]{1,2,0:T(8,128)}, f32[16,588,588]{1,2,0:T(8,128)S(1)}, u32[]{:S(2)}) copy-start(f32[16,588,588]{1,2,0:T(8,128)S(1)} %get-tuple-element.680) | copy-start | bytes 66382852 | tf_op jit(solution)/shard_map/while
  226.9 8.0 %copy-start = (f32[16,588,588]{1,2,0:T(8,128)}, f32[16,588,588]{1,2,0:T(8,128)S(1)}, u32[]{:S(2)}) copy-start(f32[16,588,588]{1,2,0:T(8,128)S(1)} %get-tuple-element.680) | copy-start | bytes 66382852 | tf_op jit(solution)/shard_map/while
  282.6 20.5 %copy-start.37 = (f32[384]{0:T(512)}, f32[384]{0:T(512)S(1)}, u32[]{:S(2)}) copy-start(f32[384]{0:T(512)S(1)} %get-tuple-element.494) | copy-start | bytes 4612
  285.6 17.5 %copy-start.4 = (f32[1176,384]{1,0:T(8,128)}, f32[1176,384]{1,0:T(8,128)S(1)}, u32[]{:S(2)}) copy-start(f32[1176,384]{1,0:T(8,128)S(1)} %get-tuple-element.559) | copy-start | bytes 5419012
  285.6 17.5 %copy-start.27 = (f32[1176]{0:T(1024)}, f32[1176]{0:T(1024)S(1)}, u32[]{:S(2)}) copy-start(f32[1176]{0:T(1024)S(1)} %broadcast_multiply_fusion.5) | copy-start | bytes 14116
  286.0 17.1 %copy-start.33 = (f32[1176]{0:T(1024)}, f32[1176]{0:T(1024)S(1)}, u32[]{:S(2)}) copy-start(f32[1176]{0:T(1024)S(1)} %add_rsqrt_fusion.1) | copy-start | bytes 14116
  291.9 8.1 %copy-start.51 = (f32[1176,1536]{1,0:T(8,128)}, f32[1176,1536]{1,0:T(8,128)S(1)}, u32[]{:S(2)}) copy-start(f32[1176,1536]{1,0:T(8,128)S(1)} %get-tuple-element.562) | copy-start | bytes 21676036
  466.2 6.3 copy-start.14
  480.4 11.0 %all-to-all-start = ((f32[8,16,3]{1,2,0:T(4,128)}), f32[8,16,3]{1,2,0:T(4,128)S(1)}, u32[]{:S(2)}, u32[]{:S(2)}) async-start(f32[8,16,3]{1,2,0:T(4,128)} %copy.442), calls=%async_computation | async-start | bytes 32768 | tf_op jit(solution)/shard_map/all_to_all | solution.py:38
  491.5 12.0 %all-to-all-start.11 = ((f32[16,1,3]{2,1,0:T(1,128)}), f32[16,1,3]{2,1,0:T(1,128)S(1)}, u32[]{:S(2)}, u32[]{:S(2)}) async-start(f32[16,1,3]{2,1,0:T(1,128)} %bitcast.57), calls=%async_computation.11 | async-start | bytes 16384 | tf_op jit(solution)/shard_map/all_to_all | solution.py:45
  503.5 10.9 %all-to-all-start.1 = ((f32[16,1,3]{2,1,0:T(1,128)}), f32[16,1,3]{2,1,0:T(1,128)S(1)}, u32[]{:S(2)}, u32[]{:S(2)}) async-start(f32[16,1,3]{2,1,0:T(1,128)} %bitcast.53), calls=%async_computation.1 | async-start | bytes 16384 | tf_op jit(solution)/shard_map/all_to_all | solution.py:45
  514.4 10.3 %all-to-all-start.4 = ((f32[8,16,6]{1,2,0:T(8,128)}), f32[8,16,6]{1,2,0:T(8,128)S(1)}, u32[]{:S(2)}, u32[]{:S(2)}) async-start(f32[8,16,6]{1,2,0:T(8,128)} %copy.451), calls=%async_computation.4 | async-start | bytes 65536 | tf_op jit(solution)/shard_map/all_to_all | solution.py:38
  524.8 29.6 %all-to-all-start.2 = ((f32[8,16,3,1153]{3,1,2,0:T(8,128)}), f32[8,16,3,1153]{3,1,2,0:T(8,128)}, u32[]{:S(2)}, u32[]{:S(2)}) async-start(f32[8,16,3,1153]{3,1,2,0:T(8,128)} %copy.449), calls=%async_computation.2 | async-start | bytes 3932160 | tf_op jit(solution)/shard_map/all_to_all | solution.py:38
  536.2 22.8 %copy-start.22 = (bf16[1176,384,1,1]{1,0,2,3:T(8,128)(2,1)S(1)}, bf16[1176,384,1,1]{1,0,2,3:T(8,128)(2,1)}, u32[]{:S(2)}) copy-start(bf16[1176,384,1,1]{1,0,2,3:T(8,128)(2,1)} %reshape.529) | copy-start | bytes 2709508
  554.3 14.7 %all-to-all-start.5 = ((f32[16,1,6]{2,1,0:T(1,128)}), f32[16,1,6]{2,1,0:T(1,128)S(1)}, u32[]{:S(2)}, u32[]{:S(2)}) async-start(f32[16,1,6]{2,1,0:T(1,128)} %bitcast.55), calls=%async_computation.5 | async-start | bytes 16384 | tf_op jit(solution)/shard_map/all_to_all | solution.py:45
  559.0 7.1 copy-start.36
  569.0 14.7 %all-to-all-start.3 = ((f32[16,3,1153]{2,1,0:T(4,128)}), f32[16,3,1153]{2,1,0:T(4,128)S(1)}, u32[]{:S(2)}, u32[]{:S(2)}) async-start(f32[16,3,1153]{2,1,0:T(4,128)} %copy.450), calls=%async_computation.3 | async-start | bytes 655360 | tf_op jit(solution)/shard_map/all_to_all | solution.py:45
  584.4 42.6 %all-to-all-start.8 = ((f32[8,16,12,385]{3,1,2,0:T(8,128)}), f32[8,16,12,385]{3,1,2,0:T(8,128)}, u32[]{:S(2)}, u32[]{:S(2)}) async-start(f32[8,16,12,385]{3,1,2,0:T(8,128)} %copy.464), calls=%async_computation.8 | async-start | bytes 6291456 | tf_op jit(solution)/shard_map/all_to_all | solution.py:38
  619.1 12.3 %copy-start.44 = (bf16[384]{0:T(512)(128)(2,1)S(1)}, bf16[384]{0:T(512)(128)(2,1)}, u32[]{:S(2)}) copy-start(bf16[384]{0:T(512)(128)(2,1)} %get-tuple-element.536) | copy-start | bytes 2308
  619.1 12.9 %copy-start.18 = (bf16[1536,385]{1,0:T(8,128)(2,1)S(1)}, bf16[1536,385]{1,0:T(8,128)(2,1)}, u32[]{:S(2)}) copy-start(bf16[1536,385]{1,0:T(8,128)(2,1)} %reshape.526) | copy-start | bytes 3548164
  627.0 42.3 %all-to-all-start.6 = ((f32[8,16,3,1923]{3,1,2,0:T(8,128)}), f32[8,16,3,1923]{3,1,2,0:T(8,128)}, u32[]{:S(2)}, u32[]{:S(2)}) async-start(f32[8,16,3,1923]{3,1,2,0:T(8,128)} %copy.460), calls=%async_computation.6 | async-start | bytes 6291456 | tf_op jit(solution)/shard_map/all_to_all | solution.py:38
  669.2 16.0 %all-to-all-start.9 = ((f32[16,12,385]{2,1,0:T(8,128)}), f32[16,12,385]{2,1,0:T(8,128)S(1)}, u32[]{:S(2)}, u32[]{:S(2)}) async-start(f32[16,12,385]{2,1,0:T(8,128)} %copy.465), calls=%async_computation.9 | async-start | bytes 1048576 | tf_op jit(solution)/shard_map/all_to_all | solution.py:45
  685.2 20.2 %all-to-all-start.7 = ((f32[16,3,1923]{2,1,0:T(4,128)}), f32[16,3,1923]{2,1,0:T(4,128)S(1)}, u32[]{:S(2)}, u32[]{:S(2)}) async-start(f32[16,3,1923]{2,1,0:T(4,128)} %copy.461), calls=%async_computation.7 | async-start | bytes 1048576 | tf_op jit(solution)/shard_map/all_to_all | solution.py:45
  (37 other events, 140.8 us)
Sparse Core Ops, SparseCore 0:
  11.6 66.4 all-gather.7
  81.6 62.7 all-gather.5
where the time goes:
time: 723 us; the launch traced here: 715 us
  matrix products  181 us (25%)
  local copies, waits for them, and re-layouts  170 us (24%)
  blocking collectives  130 us (18%)
  other arithmetic  84.1 us (12%)
  waiting for transfers between devices  63 us (9%)
  starting transfers between devices  61.6 us (9%)
  between operations  15.4 us (2%)
  loops' own time  8.93 us (1%)
    unnamed x1, blocking collectives  67.7 us
    all_gather x1, blocking collectives, in_one_piece(): whole = lax.all_gather(both, axis, axis=dim, tiled=True)  62.5 us
    all_to_all x6, waiting for transfers between devices, summed_on_arrival(): lax.all_to_all(blocks, axis, split_axis=0, concat_axis=0, tiled=True)  45.9 us
    all_to_all x6, starting transfers between devices, summed_rows(): return jnp.sum(lax.all_to_all(own, far, 0, 0, tiled=True), axis=0)  35.2 us
    dot_general x2, matrix products, attend_backward(): jnp.einsum('qhd,khd->hqk', slot_grad, slot_value, preferred_element_type=...  33 us
    convert_element_type x2, other arithmetic, attend_backward(): grad_scores = (probs * (grad_probs - row_dot)).astype(jnp.bfloat16)  32.5 us
    dot_general x2, matrix products, attend_backward(): jnp.einsum('hqk,qhd->khd', probs_again, slot_grad, preferred_element_type...  28.6 us
    dot_general x4, matrix products, masked_scores(): jnp.einsum('qhd,khd->hqk', query_heads, key_heads, preferred_element_type...  28.4 us
  transfers between devices with their start and end apart: 14, of which 8 were waited for; matrix products, arithmetic and copies ran while one was open for 30% of the time, Pallas kernels for 0%

commit v1 on v0

v1 whole, which is shorter than its diff:
```python
import math

import jax
import jax.numpy as jnp
from jax import lax
from jax.experimental import pallas as pl
from jax.experimental.pallas import tpu as pltpu
from jax.sharding import Mesh
from jax.sharding import PartitionSpec as P

HEADS = 16
HEAD = 24
FRAME = 196
WIDE = 640
EPSILON = 1e-05
NEGATIVE = -1e30
bf16 = jnp.bfloat16
f32 = jnp.float32
FORWARD_BLOCKS = ((0, 128, 208), (128, 384, 400), (384, 640, 592))
BACKWARD_BLOCKS = ((0, 128, 256), (128, 384, 512), (384, 592, 640))


def dot(left, right, over):
    return lax.dot_general(left, right, (((over[0],), (over[1],)), ((), ())), preferred_element_type=f32)


def norm_parts(values):
    centred = values - jnp.mean(values, axis=-1, keepdims=True)
    inverse = lax.rsqrt(jnp.mean(centred * centred, axis=-1, keepdims=True) + EPSILON)
    return centred * inverse, inverse


def three_parts(values):
    high = values.astype(bf16).astype(f32)
    rest = values - high
    middle = rest.astype(bf16).astype(f32)
    return high, middle, rest - middle


def rows_of(rows, width):
    index = lax.broadcasted_iota(jnp.int32, (8, width), 0)
    out = jnp.zeros((8, width), f32)
    for k, row in enumerate(rows):
        out = jnp.where(index == k, row, out)
    return out


def mask_rows(counts_ref, slot):
    lane = lax.broadcasted_iota(jnp.int32, (1, WIDE), 1)
    first_end = counts_ref[slot, 0]
    second_end = first_end + counts_ref[slot, 1]
    third_end = second_end + counts_ref[slot, 2]
    group = [
        (f >= first_end).astype(jnp.int32) + (f >= second_end).astype(jnp.int32) + (f >= third_end).astype(jnp.int32)
        for f in range(3)
    ]
    hidden = []
    for f in range(3):
        row = jnp.full((1, WIDE), NEGATIVE, f32)
        for k in range(f + 1):
            seen = jnp.where(group[f] == group[k], 0.0, NEGATIVE).astype(f32)
            row = jnp.where((lane >= FRAME * k) & (lane < FRAME * (k + 1)), seen, row)
        hidden.append(row)
    frame = [((lane >= FRAME * f) & (lane < FRAME * (f + 1))).astype(f32) for f in range(3)]
    return hidden, frame


def forward_attention(counts_ref, tokens_ref, weight_ref, bias_ref, gain_ref, offset_ref,
                      mixed_ref, query_ref, key_ref, value_ref, first_ref, projected_ref, mixed_scratch):
    slot = pl.program_id(0)
    span, width = tokens_ref.shape[1:]
    scale = math.log2(math.e) / math.sqrt(HEAD)
    normed, _ = norm_parts(tokens_ref[0].astype(f32))
    first_ref[...] = jnp.zeros_like(first_ref)
    first_ref[0:span, :] = (normed * gain_ref[...] + offset_ref[...]).astype(bf16)
    ones = jnp.where(lax.broadcasted_iota(jnp.int32, (WIDE, 16), 1) == 0, 1.0, 0.0).astype(bf16)
    bias_rows = jnp.broadcast_to(bias_ref[...], (16, 3 * width)).astype(bf16)
    projected_ref[...] = dot(weight_ref[...], first_ref[...], (0, 1)) + dot(bias_rows, ones, (0, 1))
    hidden, frame = mask_rows(counts_ref, slot)
    one = jnp.ones((1, WIDE), f32)
    query_more = rows_of(frame, WIDE)
    key_more = rows_of(hidden + [one, one, one], WIDE)
    value_more = rows_of([one, one, one], WIDE)

    def head_step(h, _):
        at = pl.multiple_of(h * HEAD, 8)
        to = pl.multiple_of(h * 32, 32)
        query = jnp.concatenate([projected_ref[pl.ds(at, HEAD), :] * scale, query_more], 0)
        key = jnp.concatenate([projected_ref[pl.ds(at + width, HEAD), :], key_more], 0).astype(bf16)
        value = jnp.concatenate([projected_ref[pl.ds(at + 2 * width, HEAD), :], value_more], 0).astype(bf16)
        query_low = query.astype(bf16)
        logs = []
        for low, high, keys in FORWARD_BLOCKS:
            scores = dot(key[:, :keys], query_low[:, low:high], (0, 0))
            peak = jnp.max(scores, axis=0, keepdims=True)
            weights = jnp.exp2(scores - peak).astype(bf16)
            got = dot(value[:, :keys], weights, (1, 0))
            total = got[HEAD : HEAD + 1]
            mixed_scratch[pl.ds(at, HEAD), low:high] = got[:HEAD] / total
            logs.append(peak + jnp.log2(total))
        log_total = jnp.concatenate(logs, 1)
        high_part, middle_part, low_part = three_parts(-log_total)
        zero = jnp.zeros((1, WIDE), f32)
        log_rows = rows_of([zero, zero, zero, high_part, middle_part, low_part], WIDE)
        query_ref[0, pl.ds(to, 32), :] = (query + jnp.concatenate([jnp.zeros((HEAD, WIDE), f32), log_rows], 0)).astype(bf16)
        key_ref[0, pl.ds(to, 32), :] = key
        value_ref[0, pl.ds(to, 32), :] = value
        return 0

    lax.fori_loop(0, HEADS, head_step, 0, unroll=2)
    mixed_ref[0] = mixed_scratch[...].astype(bf16)


def run_forward(counts, tokens, weight, bias, gain, offset):
    slots, span, width = tokens.shape
    whole = lambda shape: pl.BlockSpec(shape, lambda s: (0,) * len(shape))
    per_slot = lambda rows: pl.BlockSpec((1, rows, WIDE), lambda s: (s, 0, 0))
    return pl.pallas_call(
        forward_attention,
        grid=(slots,),
        in_specs=[
            pl.BlockSpec(memory_space=pltpu.SMEM),
            pl.BlockSpec((1, span, width), lambda s: (s, 0, 0)),
            whole((width, 3 * width)),
            whole((1, 3 * width)),
            whole((1, width)),
            whole((1, width)),
        ],
        out_specs=[per_slot(width), per_slot(512), per_slot(512), per_slot(512)],
        out_shape=[jax.ShapeDtypeStruct((slots, rows, WIDE), bf16) for rows in (width, 512, 512, 512)],
        scratch_shapes=[pltpu.VMEM((WIDE, width), bf16), pltpu.VMEM((3 * width, WIDE), f32), pltpu.VMEM((width, WIDE), f32)],
        compiler_params=pltpu.CompilerParams(vmem_limit_bytes=56 * 2**20),
        name="attention_forward",
    )(counts, tokens, weight, bias, gain, offset)


def feed_forward(tokens_ref, mixed_ref, cotangent_ref, out_w_ref, up_w_ref, down_w_ref, out_b_ref, gain_ref, offset_ref, up_b_ref, down_b_ref,
                 output_ref, grad_resid_ref, grad_mixed_ref, grad_out_ref, grad_up_ref, grad_down_ref, vector_ref, up_vector_ref):
    slot = pl.program_id(0)
    span, width = tokens_ref.shape[1:]
    hidden = up_w_ref.shape[1]
    chunk = 384

    @pl.when(slot == 0)
    def _():
        grad_out_ref[...] = jnp.zeros_like(grad_out_ref)
        grad_up_ref[...] = jnp.zeros_like(grad_up_ref)
        grad_down_ref[...] = jnp.zeros_like(grad_down_ref)
        vector_ref[...] = jnp.zeros_like(vector_ref)
        up_vector_ref[...] = jnp.zeros_like(up_vector_ref)

    mixed = mixed_ref[0]
    mixed = mixed[:, :span]
    resid = tokens_ref[0].astype(f32) + dot(mixed, out_w_ref[...], (0, 0)) + out_b_ref[...]
    normed, inverse = norm_parts(resid)
    second = (normed * gain_ref[...] + offset_ref[...]).astype(bf16)
    grad_branch = cotangent_ref[0]
    result = resid + down_b_ref[...]
    grad_second = jnp.zeros((span, width), f32)
    root = math.sqrt(2.0 / math.pi)
    for at in range(0, hidden, chunk):
        cols = slice(at, at + chunk)
        up = dot(second, up_w_ref[:, cols], (1, 0)) + up_b_ref[:, cols]
        square = up * up
        tanh = jnp.tanh(up * (root + (root * 0.044715) * square))
        half = 0.5 + 0.5 * tanh
        activated = (up * half).astype(bf16)
        slope = half + (up * (2.0 * half * (1.0 - half))) * (root + (3 * root * 0.044715) * square)
        result += dot(activated, down_w_ref[cols, :], (1, 0))
        grad_up = (dot(grad_branch, down_w_ref[cols, :], (1, 1)) * slope).astype(bf16)
        grad_down_ref[cols, :] += dot(activated, grad_branch, (0, 0))
        grad_up_ref[:, cols] += dot(second, grad_up, (0, 0))
        up_vector_ref[:, cols] += jnp.sum(grad_up.astype(f32), axis=0, keepdims=True)
        grad_second += dot(grad_up, up_w_ref[:, cols], (1, 1))
    output_ref[0] = result.astype(bf16)
    scaled = grad_second * gain_ref[...]
    mean_one = jnp.mean(scaled, axis=-1, keepdims=True)
    mean_two = jnp.mean(scaled * normed, axis=-1, keepdims=True)
    grad_full = grad_branch.astype(f32)
    grad_resid = grad_full + inverse * (scaled - mean_one - normed * mean_two)
    grad_resid_ref[0] = grad_resid
    attended = grad_resid.astype(bf16)
    grad_out_ref[...] += dot(mixed, attended, (1, 0))
    grad_mixed_ref[0] = jnp.zeros_like(grad_mixed_ref[0])
    grad_mixed_ref[0, :, :span] = dot(out_w_ref[...], attended, (1, 1)).astype(bf16)
    vector_ref[0:1] += jnp.sum(attended.astype(f32), axis=0, keepdims=True)
    vector_ref[1:2] += jnp.sum(grad_second * normed, axis=0, keepdims=True)
    vector_ref[2:3] += jnp.sum(grad_second, axis=0, keepdims=True)
    vector_ref[3:4] += jnp.sum(grad_full, axis=0, keepdims=True)


def run_feed_forward(tokens, mixed, cotangent, out_w, up_w, down_w, out_b, gain, offset, up_b, down_b):
    slots, span, width = tokens.shape
    hidden = up_w.shape[1]
    whole = lambda *shape: pl.BlockSpec(shape, lambda s: (0,) * len(shape))
    rows = pl.BlockSpec((1, span, width), lambda s: (s, 0, 0))
    turned = pl.BlockSpec((1, width, WIDE), lambda s: (s, 0, 0))
    return pl.pallas_call(
        feed_forward,
        grid=(slots,),
        in_specs=[rows, turned, rows, whole(width, width), whole(width, hidden), whole(hidden, width), whole(1, width),
                  whole(1, width), whole(1, width), whole(1, hidden), whole(1, width)],
        out_specs=[rows, rows, turned, whole(width, width), whole(width, hidden), whole(hidden, width), whole(8, width), whole(1, hidden)],
        out_shape=[
            jax.ShapeDtypeStruct((slots, span, width), bf16),
            jax.ShapeDtypeStruct((slots, span, width), f32),
            jax.ShapeDtypeStruct((slots, width, WIDE), bf16),
            jax.ShapeDtypeStruct((width, width), f32),
            jax.ShapeDtypeStruct((width, hidden), f32),
            jax.ShapeDtypeStruct((hidden, width), f32),
            jax.ShapeDtypeStruct((8, width), f32),
            jax.ShapeDtypeStruct((1, hidden), f32),
        ],
        compiler_params=pltpu.CompilerParams(vmem_limit_bytes=56 * 2**20),
        name="feed_forward",
    )(tokens, mixed, cotangent, out_w, up_w, down_w, out_b, gain, offset, up_b, down_b)


def backward_attention(tokens_ref, query_ref, key_ref, value_ref, mixed_ref, grad_mixed_ref, grad_resid_ref, weight_ref, gain_ref, offset_ref,
                       input_grad_ref, grad_weight_ref, grad_bias_ref, vector_ref, first_ref, turned_ref):
    slot = pl.program_id(0)
    span, width = tokens_ref.shape[1:]

    @pl.when(slot == 0)
    def _():
        grad_weight_ref[...] = jnp.zeros_like(grad_weight_ref)
        grad_bias_ref[...] = jnp.zeros_like(grad_bias_ref)
        vector_ref[...] = jnp.zeros_like(vector_ref)

    normed, inverse = norm_parts(tokens_ref[0].astype(f32))
    first_ref[...] = jnp.zeros_like(first_ref)
    first_ref[0:span, :] = (normed * gain_ref[...] + offset_ref[...]).astype(bf16)

    def head_step(pair, _):
        for part in range(2):
            h = pair * 2 + part
            to = pl.multiple_of(h * 32, 32)
            at = pl.multiple_of(h * HEAD, 8)
            query = query_ref[0, pl.ds(to, 32), :]
            key = key_ref[0, pl.ds(to, 32), :]
            value = value_ref[0, pl.ds(to, 32), :]
            both = pl.multiple_of(pair * 48, 16)
            grad = grad_mixed_ref[0, pl.ds(both, 48), :].astype(f32)[HEAD * part : HEAD * part + HEAD]
            mixed = mixed_ref[0, pl.ds(both, 48), :].astype(f32)[HEAD * part : HEAD * part + HEAD]
            shift = jnp.sum(grad * mixed, axis=0, keepdims=True)
            grad = jnp.concatenate([grad, rows_of(three_parts(-shift), WIDE)], 0).astype(bf16)
            grad_q = []
            grad_k = jnp.zeros((32, WIDE), f32)
            grad_v = jnp.zeros((32, WIDE), f32)
            for low, high, keys in BACKWARD_BLOCKS:
                probs = jnp.exp2(dot(query[:, low:high], key[:, :keys], (0, 0)))
                grad_scores = (probs * dot(grad[:, low:high], value[:, :keys], (0, 0))).astype(bf16)
                probs_low = probs.astype(bf16)
                more_v = dot(grad[:, low:high], probs_low, (1, 0))
                more_k = dot(query[:, low:high], grad_scores, (1, 0))
                grad_q.append(dot(key[:, :keys], grad_scores, (1, 1)))
                if keys < WIDE:
                    blank = jnp.zeros((32, WIDE - keys), f32)
                    more_v = jnp.concatenate([more_v, blank], 1)
                    more_k = jnp.concatenate([more_k, blank], 1)
                grad_v += more_v
                grad_k += more_k
            grad_q.append(jnp.zeros((32, WIDE - 592), f32))
            grad_q = jnp.concatenate(grad_q, 1)
            turned_ref[pl.ds(at, HEAD), :] = grad_q[:HEAD] * (1.0 / math.sqrt(HEAD))
            turned_ref[pl.ds(at + width, HEAD), :] = grad_k[:HEAD] * math.log(2.0)
            turned_ref[pl.ds(at + 2 * width, HEAD), :] = grad_v[:HEAD]
        return 0

    lax.fori_loop(0, HEADS // 2, head_step, 0)
    turned = turned_ref[...].astype(bf16)
    grad_bias_ref[...] += jnp.sum(turned.astype(f32), axis=1, keepdims=True)
    grad_weight_ref[...] += dot(first_ref[...], turned, (0, 1))
    grad_first = dot(turned, weight_ref[...], (0, 1))[:span]
    scaled = grad_first * gain_ref[...]
    mean_one = jnp.mean(scaled, axis=-1, keepdims=True)
    mean_two = jnp.mean(scaled * normed, axis=-1, keepdims=True)
    input_grad_ref[0] = grad_resid_ref[0] + inverse * (scaled - mean_one - normed * mean_two)
    vector_ref[0:1] += jnp.sum(grad_first * normed, axis=0, keepdims=True)
    vector_ref[1:2] += jnp.sum(grad_first, axis=0, keepdims=True)


def run_backward(tokens, query, key, value, mixed, grad_mixed, grad_resid, weight, gain, offset):
    slots, span, width = tokens.shape
    whole = lambda *shape: pl.BlockSpec(shape, lambda s: (0,) * len(shape))
    rows = pl.BlockSpec((1, span, width), lambda s: (s, 0, 0))
    turned = lambda n: pl.BlockSpec((1, n, WIDE), lambda s: (s, 0, 0))
    return pl.pallas_call(
        backward_attention,
        grid=(slots,),
        in_specs=[rows, turned(512), turned(512), turned(512), turned(width), turned(width), rows, whole(width, 3 * width), whole(1, width), whole(1, width)],
        out_specs=[rows, whole(width, 3 * width), whole(3 * width, 1), whole(8, width)],
        out_shape=[
            jax.ShapeDtypeStruct((slots, span, width), f32),
            jax.ShapeDtypeStruct((width, 3 * width), f32),
            jax.ShapeDtypeStruct((3 * width, 1), f32),
            jax.ShapeDtypeStruct((8, width), f32),
        ],
        scratch_shapes=[pltpu.VMEM((WIDE, width), bf16), pltpu.VMEM((3 * width, WIDE), f32)],
        compiler_params=pltpu.CompilerParams(vmem_limit_bytes=56 * 2**20),
        name="attention_backward",
    )(tokens, query, key, value, mixed, grad_mixed, grad_resid, weight, gain, offset)


ALL = ("wide_0", "wide_1", "wide_2", "narrow")
DEVICES = 128


def row(values):
    return values.astype(f32)[None]


def shards(tokens, item_frames, ln1_gain, ln1_bias, qkv_weight, qv_bias, out_weight, out_bias, ln2_gain, ln2_bias,
           up_weight, up_bias, down_weight, down_bias, cotangent):
    width = tokens.shape[2]
    own = width // DEVICES
    column = lambda v: v.reshape(-1, 1)
    early = jnp.concatenate([qkv_weight, column(ln1_gain), column(ln1_bias), qv_bias.reshape(own, 2)], 1)
    early = jnp.broadcast_to(early[None], (DEVICES, *early.shape))
    early = lax.all_to_all(early, ALL, 0, 0, tiled=True).reshape(width, -1)
    qkv = early[:, : 3 * width]
    gain_one, offset_one = early[:, 3 * width], early[:, 3 * width + 1]
    qv = early[:, 3 * width + 2 :].reshape(-1)
    wide = lax.all_gather(
        jnp.concatenate([out_weight, up_weight, column(out_bias), column(ln2_gain), column(ln2_bias), column(down_bias)], 1),
        ALL, axis=0, tiled=True)
    tall = lax.all_gather(jnp.concatenate([down_weight, column(up_bias)], 1), ALL, axis=0, tiled=True)
    bias = jnp.concatenate([qv[:width], jnp.zeros((width,), qv.dtype), qv[width:]])
    mixed, query, key, value = run_forward(item_frames, tokens, qkv, row(bias), row(gain_one), row(offset_one))
    hidden = up_weight.shape[1]
    out_w, up_w = wide[:, :width], wide[:, width : width + hidden]
    out_b, gain_two, offset_two, down_b = (row(wide[:, width + hidden + k]) for k in range(4))
    down_w, up_b = tall[:, :width], row(tall[:, width])
    output, grad_resid, grad_mixed, grad_out, grad_up, grad_down, vectors, up_vector = run_feed_forward(
        tokens, mixed, cotangent, out_w, up_w, down_w, out_b, gain_two, offset_two, up_b, down_b)

    def spread(parts, rows):
        both = jnp.concatenate(parts, 1).astype(bf16)
        both = both.reshape(DEVICES, rows, both.shape[1])
        return jnp.sum(lax.all_to_all(both, ALL, 0, 0, tiled=True).astype(f32), 0)

    wide_sum = spread([grad_out, grad_up, vectors[:4].T], own)
    tall_sum = spread([grad_down, up_vector.T], 4 * own)
    input_grad, grad_qkv, grad_bias, vectors_one = run_backward(
        tokens, query, key, value, mixed, grad_mixed, grad_resid, qkv, row(gain_one), row(offset_one))
    grad_bias = grad_bias[:, 0]
    grad_qv = jnp.concatenate([grad_bias[:width], grad_bias[2 * width :]]).reshape(width, 2)
    first_sum = spread([grad_qkv, vectors_one[:2].T, grad_qv], own)
    at = width + hidden
    return (
        output,
        input_grad,
        first_sum[:, 3 * width],
        first_sum[:, 3 * width + 1],
        first_sum[:, : 3 * width],
        first_sum[:, 3 * width + 2 :].reshape(-1),
        wide_sum[:, :width],
        wide_sum[:, at],
        wide_sum[:, at + 1],
        wide_sum[:, at + 2],
        wide_sum[:, width:at],
        tall_sum[:, width],
        tall_sum[:, :width],
        wide_sum[:, at + 3],
    )


def solution(mesh):
    split = Mesh(mesh.devices.reshape(4, 4, 2, mesh.shape["narrow"]), ALL)
    by_rank = lambda n: P(ALL, *([None] * (n - 1)))
    return jax.shard_map(
        shards,
        mesh=split,
        in_specs=tuple(by_rank(n) for n in (3, 2, 1, 1, 2, 1, 2, 1, 1, 1, 2, 1, 2, 1, 3)),
        out_specs=tuple(by_rank(n) for n in (3, 3, 1, 1, 2, 1, 2, 1, 1, 1, 2, 1, 2, 1)),
        check_vma=False,
    )
```

time: 723 us -> 352 us (0.49)
  matrix products: 181 us -> 0 us
  blocking collectives: 130 us -> 0 us
  local copies, waits for them, and re-layouts: 170 us -> 57.5 us
  Pallas kernels: 0 us -> 107 us
  other arithmetic: 84.1 us -> 21.6 us
  waiting for transfers between devices: 63 us -> 119 us
  starting transfers between devices: 61.6 us -> 28.3 us
  loops' own time: 8.93 us -> 0 us
    dot_general x26 -> x0, matrix products: 181 us -> none  [the longest x2 33 us: attend_backward(): jnp.einsum('qhd,khd->hqk', slot_grad, slot_value, preferred_element_type=...]
    pallas_call x0 -> x3, Pallas kernels: none -> 107 us  [the longest x1 43.5 us: run_backward(): pl.pallas_call(backward_attention, grid=(slots,), in_specs=[rows, turned(...]
    unnamed x1 -> x0, blocking collectives: 67.7 us -> none
    all_gather x1 -> x0, blocking collectives: 62.5 us -> none  [in_one_piece(): whole = lax.all_gather(both, axis, axis=dim, tiled=True)]
    all_gather x2, waiting for transfers between devices: 0.02 us -> 53.3 us  [the longest x1 53.3 us: shards(): lax.all_gather(jnp.concatenate([out_weight, up_weight, column(out_bias),...]
    convert_element_type x8 -> x4, other arithmetic: 36.4 us -> 1.32 us  [row(): return values.astype(f32)[None]]
    all_to_all x12 -> x4, starting transfers between devices: 61.5 us -> 28.2 us  [the longest x3 17.7 us: spread(): return jnp.sum(lax.all_to_all(both, ALL, 0, 0, tiled=True).astype(f32), 0)]
    reshape x22 -> x10, local copies, waits for them, and re-layouts: 40.8 us -> 7.53 us  [the longest x7 5.35 us: shards(): column = lambda v: v.reshape(-1, 1)]
  transfers between devices with their start and end apart: 14 -> 6, of which waited for: 8 -> 5; matrix products, arithmetic and copies ran while one was open for 30% -> 15% of each run, Pallas kernels for 0% -> 11%
where the time goes in v1:
time: 352 us; the launch traced here: 348 us
  waiting for transfers between devices  119 us (34%)
  Pallas kernels  107 us (30%)
  local copies, waits for them, and re-layouts  57.5 us (16%)
  starting transfers between devices  28.3 us (8%)
  other arithmetic  21.6 us (6%)
  between operations  14.2 us (4%)
    all_gather x1, waiting for transfers between devices, shards(): lax.all_gather(jnp.concatenate([out_weight, up_weight, column(out_bias),...  53.3 us
    all_to_all x3, waiting for transfers between devices, spread(): return jnp.sum(lax.all_to_all(both, ALL, 0, 0, tiled=True).astype(f32), 0)  46.9 us
    pallas_call x1, Pallas kernels, run_backward(): pl.pallas_call(backward_attention, grid=(slots,), in_specs=[rows, turned(...  43.5 us
    pallas_call x1, Pallas kernels, run_forward(): pl.pallas_call(forward_attention, grid=(slots,), in_specs=[pl.BlockSpec(m...  39.3 us
    pallas_call x1, Pallas kernels, run_feed_forward(): pl.pallas_call(feed_forward, grid=(slots,), in_specs=[rows, turned, rows,...  24.6 us
    all_to_all x1, waiting for transfers between devices, shards(): early = lax.all_to_all(early, ALL, 0, 0, tiled=True).reshape(width, -1)  19.3 us
    all_to_all x3, starting transfers between devices, spread(): return jnp.sum(lax.all_to_all(both, ALL, 0, 0, tiled=True).astype(f32), 0)  17.7 us
    concatenate x12, local copies, waits for them, and re-layouts, spread(): both = jnp.concatenate(parts, 1).astype(bf16)  17.1 us
  transfers between devices with their start and end apart: 6, of which 5 were waited for; matrix products, arithmetic and copies ran while one was open for 15% of the time, Pallas kernels for 11%

profile of v1, /device:TPU:2, one launch (start us, length us, event | category | flops | bytes accessed | tf_op | source)
XLA Modules:
  0.0 348.4 jit_solution(13627748201926755866)
XLA Ops:
  8.0 1.3 maximum_bitcast_fusion
  12.5 1.4 concatenate.67
  17.0 1.4 broadcast_in_dim.4
  18.4 10.5 %all-to-all-start = ((bf16[128,3,1156]{2,1,0:T(4,128)(2,1)}), bf16[128,3,1156]{2,1,0:T(4,128)(2,1)S(1)}, u32[]{:S(2)}, u32[]{:S(2)}) async-start(bf16[128,3,1156]{2,1,0:T(4,128)(2,1)} %broadcast_in_dim.4), calls=%async_computation | async-start | bytes 2621440 | tf_op jit(solution)/shard_map/all_to_all | solution.py:320
  31.0 19.3 %all-to-all-done = bf16[128,3,1156]{2,1,0:T(4,128)(2,1)S(1)} async-done(((bf16[128,3,1156]{2,1,0:T(4,128)(2,1)}), bf16[128,3,1156]{2,1,0:T(4,128)(2,1)S(1)}, u32[]{:S(2)}, u32[]{:S(2)}) %all-to-all-start) | async-done | bytes 887840 | tf_op jit(solution)/shard_map/all_to_all | solution.py:320
  54.5 39.3 %attention_forward.1 = (bf16[2,384,640]{2,1,0:T(8,128)(2,1)}, bf16[2,512,640]{2,1,0:T(8,128)(2,1)}, bf16[2,512,640]{2,1,0:T(8,128)(2,1)}, bf16[2,512,640]{2,1,0:T(8,128)(2,1)}) custom-call(s32[2,3]{1,0:T(2,128)} %counts_ref.1, bf16[2,588,384]{2,1,0:T(8,128)(2,1)} %copy.71.tokens_ref, bf16[384,1152]{1,0:T(8,128)(2,1)} %slice.127.weight_ref, ...), custom_call_target="tpu_custom_call" | custom-call | tf_op jit(solution)/shard_map/attention_forward/pallas_call | solution.py:118
  93.8 2.8 reshape.233
  96.6 1.2 slice.134.down_w_ref
  98.6 53.3 %all-gather.5.cloned.1.call-done = bf16[128,3,1924]{2,1,0:T(4,128)(2,1)} async-done(((bf16[1,3,1924]{2,1,0:T(4,128)(2,1)}), bf16[128,3,1924]{2,1,0:T(4,128)(2,1)}) %all-gather.5.cloned.1.call-update) | async-done | bytes 1477648 | tf_op jit(solution)/shard_map/all_gather | solution.py:324
  151.8 3.9 %reshape.231 = bf16[384,1924]{1,0:T(8,128)(2,1)S(1)} reshape(bf16[128,3,1924]{2,1,0:T(4,128)(2,1)} %all-gather.5.cloned.1.call-done) | data formatting | bytes 2955264
  160.2 24.6 %feed_forward.1 = (bf16[2,588,384]{2,1,0:T(8,128)(2,1)}, f32[2,588,384]{2,1,0:T(8,128)}, bf16[2,384,640]{2,1,0:T(8,128)(2,1)}, f32[384,384]{1,0:T(8,128)}, f32[3...) custom-call(bf16[2,588,384]{2,1,0:T(8,128)(2,1)} %copy.71.tokens_ref, ...), custom_call_target="tpu_custom_call" | custom-call | tf_op jit(solution)/shard_map/feed_forward/pallas_call | solution.py:198
  184.8 43.5 %attention_backward.1 = (f32[2,588,384]{2,1,0:T(8,128)}, f32[384,1152]{1,0:T(8,128)}, f32[1152,1]{1,0:T(8,128)}, f32[8,384]{1,0:T(8,128)}) custom-call(bf16[2,588,384]{2,1,0:T(8,128)(2,1)} %copy.71.tokens_ref, bf16[2,512,640]{2,1,0:T(8,128)(2,1)} %get-tuple-element.32.query_ref, bf16[2,512,640]{2,1,0:T(8,128)(2,1)} %get-tuple-element.33.key_ref, ...), custom_call_target="tpu_custom_call" | custom-call | tf_op jit(solution)/shard_map/attention_backward/pallas_call | solution.py:288
  231.3 1.6 convert.49
  235.1 3.5 %concatenate.75 = bf16[128,3,1156]{2,1,0:T(4,128)(2,1)} concatenate(bf16[128,3,1152]{2,1,0:T(4,128)(2,1)S(1)} %concatenate.69, bf16[128,3,2]{2,1,0:T(4,128)(2,1)S(1)} %copy.76, bf16[128,3,2]{2,1,0:T(4,128)(2,1)S(1)} %copy.77), dimensions={2} | concatenate | bytes 1775616 | tf_op jit(solution)/shard_map/concatenate | solution.py:338
  238.7 6.8 %all-to-all-start.1 = ((bf16[128,3,1156]{2,1,0:T(4,128)(2,1)}), bf16[128,3,1156]{2,1,0:T(4,128)(2,1)S(1)}, u32[]{:S(2)}, u32[]{:S(2)}) async-start(bf16[128,3,1156]{2,1,0:T(4,128)(2,1)} %concatenate.75), calls=%async_computation.1 | async-start | bytes 2621440 | tf_op jit(solution)/shard_map/all_to_all | solution.py:340
  245.5 2.8 convert.55
  248.3 2.2 concatenate.80
  251.0 1.7 pad_maximum_fusion.1
  252.7 14.1 %all-to-all-done.1 = bf16[128,3,1156]{2,1,0:T(4,128)(2,1)S(1)} async-done(((bf16[128,3,1156]{2,1,0:T(4,128)(2,1)}), bf16[128,3,1156]{2,1,0:T(4,128)(2,1)S(1)}, u32[]{:S(2)}, u32[]{:S(2)}) %all-to-all-start.1) | async-done | bytes 887840 | tf_op jit(solution)/shard_map/all_to_all | solution.py:340
  266.8 4.9 %all-to-all-start.3 = ((bf16[128,12,385]{2,1,0:T(8,128)(2,1)}), bf16[128,12,385]{2,1,0:T(8,128)(2,1)S(1)}, u32[]{:S(2)}, u32[]{:S(2)}) async-start(bf16[128,12,385]{2,1,0:T(8,128)(2,1)} %pad_maximum_fusion.1), calls=%async_computation.3 | async-start | bytes 4194304 | tf_op jit(solution)/shard_map/all_to_all | solution.py:340
  271.8 2.8 convert.53
  274.6 3.8 %concatenate.77 = bf16[128,3,1536]{2,1,0:T(4,128)(2,1)} reshape(bf16[384,1536]{1,0:T(8,128)(2,1)} %convert.53) | data formatting | bytes 2359296 | tf_op jit(solution)/shard_map/concatenate | solution.py:338
  278.3 1.8 convert.52
  280.2 1.8 concatenate.76
  283.6 1.8 copy.78
  285.4 3.5 %pad_maximum_fusion = bf16[128,3,1924]{2,1,0:T(4,128)(2,1)} fusion(bf16[128,3,4]{2,1,0:T(4,128)(2,1)S(1)} %copy.78, bf16[128,3,1536]{2,1,0:T(4,128)(2,1)} %concatenate.77, bf16[128,3,384]{2,1,0:T(4,128)(2,1)} %concatenate.76), kind=kLoop, calls=%fused_computation.3 | loop fusion | flops 4432896 | bytes 2955264 | tf_op jit(solution)/shard_map/concatenate | solution.py:338
  288.9 12.8 %all-to-all-done.3 = bf16[128,12,385]{2,1,0:T(8,128)(2,1)S(1)} async-done(((bf16[128,12,385]{2,1,0:T(8,128)(2,1)}), bf16[128,12,385]{2,1,0:T(8,128)(2,1)S(1)}, u32[]{:S(2)}, u32[]{:S(2)}) %all-to-all-start.3) | async-done | bytes 1182752 | tf_op jit(solution)/shard_map/all_to_all | solution.py:340
  301.7 6.0 %all-to-all-start.2 = ((bf16[128,3,1924]{2,1,0:T(4,128)(2,1)}), bf16[128,3,1924]{2,1,0:T(4,128)(2,1)}, u32[]{:S(2)}, u32[]{:S(2)}) async-start(bf16[128,3,1924]{2,1,0:T(4,128)(2,1)} %pad_maximum_fusion), calls=%async_computation.2 | async-start | bytes 4194304 | tf_op jit(solution)/shard_map/all_to_all | solution.py:340
  307.6 3.7 %copy.81 = f32[2,588,384]{2,0,1:T(2,128)} copy(f32[2,588,384]{2,1,0:T(8,128)} %get-tuple-element.75) | data formatting | bytes 3612672
  311.4 1.6 copy.80
  317.2 20.0 %all-to-all-done.2 = bf16[128,3,1924]{2,1,0:T(4,128)(2,1)} async-done(((bf16[128,3,1924]{2,1,0:T(4,128)(2,1)}), bf16[128,3,1924]{2,1,0:T(4,128)(2,1)}, u32[]{:S(2)}, u32[]{:S(2)}) %all-to-all-start.2) | async-done | bytes 1477664 | tf_op jit(solution)/shard_map/all_to_all | solution.py:340
  337.2 2.5 convert_reduce_fusion.1
  (72 shorter events, 32.0 us)
Async XLA Ops:
  7.2 21.7 %copy-start.1 = (bf16[2,588,384]{2,0,1:T(2,128)(2,1)S(1)}, bf16[2,588,384]{2,0,1:T(2,128)(2,1)}, u32[]{:S(2)}) copy-start(bf16[2,588,384]{2,0,1:T(2,128)(2,1)} %param.15) | copy-start | bytes 2709508
  7.2 86.6 %all-gather.7.cloned.1.call-start = ((), (), s32[]{:S(2)}) async-start(), calls=%async_computation.5 | async-start | bytes 2113536 | tf_op jit(solution)/shard_map/all_gather | solution.py:327
  9.4 142.4 %all-gather.5.cloned.1.call-start = ((), (), s32[]{:S(2)}) async-start(), calls=%async_computation.4 | async-start | bytes 2113536 | tf_op jit(solution)/shard_map/all_gather | solution.py:324
  18.4 11.6 %copy-start.2 = (bf16[2,588,384]{2,0,1:T(2,128)(2,1)S(1)}, bf16[2,588,384]{2,0,1:T(2,128)(2,1)}, u32[]{:S(2)}) copy-start(bf16[2,588,384]{2,0,1:T(2,128)(2,1)} %param.29) | copy-start | bytes 2709508
  18.4 32.0 %all-to-all-start = ((bf16[128,3,1156]{2,1,0:T(4,128)(2,1)}), bf16[128,3,1156]{2,1,0:T(4,128)(2,1)S(1)}, u32[]{:S(2)}, u32[]{:S(2)}) async-start(bf16[128,3,1156]{2,1,0:T(4,128)(2,1)} %broadcast_in_dim.4), calls=%async_computation | async-start | bytes 2621440 | tf_op jit(solution)/shard_map/all_to_all | solution.py:320
  238.7 28.2 %all-to-all-start.1 = ((bf16[128,3,1156]{2,1,0:T(4,128)(2,1)}), bf16[128,3,1156]{2,1,0:T(4,128)(2,1)S(1)}, u32[]{:S(2)}, u32[]{:S(2)}) async-start(bf16[128,3,1156]{2,1,0:T(4,128)(2,1)} %concatenate.75), calls=%async_computation.1 | async-start | bytes 2621440 | tf_op jit(solution)/shard_map/all_to_all | solution.py:340
  248.3 2.2 copy-start.3
  266.8 34.8 %all-to-all-start.3 = ((bf16[128,12,385]{2,1,0:T(8,128)(2,1)}), bf16[128,12,385]{2,1,0:T(8,128)(2,1)S(1)}, u32[]{:S(2)}, u32[]{:S(2)}) async-start(bf16[128,12,385]{2,1,0:T(8,128)(2,1)} %pad_maximum_fusion.1), calls=%async_computation.3 | async-start | bytes 4194304 | tf_op jit(solution)/shard_map/all_to_all | solution.py:340
  301.7 35.5 %all-to-all-start.2 = ((bf16[128,3,1924]{2,1,0:T(4,128)(2,1)}), bf16[128,3,1924]{2,1,0:T(4,128)(2,1)}, u32[]{:S(2)}, u32[]{:S(2)}) async-start(bf16[128,3,1924]{2,1,0:T(4,128)(2,1)} %pad_maximum_fusion), calls=%async_computation.2 | async-start | bytes 4194304 | tf_op jit(solution)/shard_map/all_to_all | solution.py:340
  307.6 3.7 %copy-start = (bf16[2,588,384]{2,1,0:T(8,128)(2,1)S(1)}, bf16[2,588,384]{2,1,0:T(8,128)(2,1)}, u32[]{:S(2)}) copy-start(bf16[2,588,384]{2,1,0:T(8,128)(2,1)} %get-tuple-element.74) | copy-start | bytes 2709508
Sparse Core Ops, SparseCore 0:
  11.6 73.9 all-gather.6
  89.1 62.6 all-gather.4

commit v2 on v1

v2 whole, which is shorter than its diff:
```python
import math

import jax
import jax.numpy as jnp
from jax import lax
from jax.experimental import pallas as pl
from jax.experimental.pallas import tpu as pltpu
from jax.sharding import Mesh
from jax.sharding import PartitionSpec as P

HEADS = 16
HEAD = 24
FRAME = 196
WIDTH = 384
HIDDEN = 1536
WIDE = 640
CHIPS = 64
EARLY_ROWS = 32
LATE_ROWS = 96
EPSILON = 1e-05
NEGATIVE = -1e30
bf16 = jnp.bfloat16
f32 = jnp.float32
FORWARD_BLOCKS = ((0, 128, 208), (128, 384, 400), (384, 640, 592))
BACKWARD_BLOCKS = ((0, 128, 256), (128, 384, 512), (384, 592, 640))
ALL = ("wide_0", "wide_1", "wide_2", "narrow")
CHIP_AXES = ("wide_0", "wide_1", "narrow")
CORE_AXIS = "wide_2"
VMEM_LIMIT = 56 * 2**20


def dot(left, right, over):
    return lax.dot_general(left, right, (((over[0],), (over[1],)), ((), ())), preferred_element_type=f32)


def norm_parts(values):
    centred = values - jnp.mean(values, axis=-1, keepdims=True)
    inverse = lax.rsqrt(jnp.mean(centred * centred, axis=-1, keepdims=True) + EPSILON)
    return centred * inverse, inverse


def two_parts(values):
    high = values.astype(bf16).astype(f32)
    return high, values - high


def three_parts(values):
    high, rest = two_parts(values)
    middle, low = two_parts(rest)
    return high, middle, low


def rows_of(rows, width, count=8):
    index = lax.broadcasted_iota(jnp.int32, (count, width), 0)
    out = jnp.zeros((count, width), f32)
    for k, row in enumerate(rows):
        out = jnp.where(index == k, row, out)
    return out


def arrival_order():
    place = lax.broadcasted_iota(jnp.int32, (WIDTH, WIDTH), 1)
    feature = lax.broadcasted_iota(jnp.int32, (WIDTH, WIDTH), 0)
    core = (place >= WIDTH // 2).astype(jnp.int32)
    rest = place - core * (WIDTH // 2)
    row = rest >> 6
    chip = rest & 63
    return (feature == 3 * (8 * (chip >> 2) + 4 * core + (chip & 3)) + row).astype(f32).astype(bf16)


def mask_rows(counts_ref, slot):
    lane = lax.broadcasted_iota(jnp.int32, (1, WIDE), 1)
    first_end = counts_ref[slot, 0]
    second_end = first_end + counts_ref[slot, 1]
    third_end = second_end + counts_ref[slot, 2]
    group = [
        (f >= first_end).astype(jnp.int32) + (f >= second_end).astype(jnp.int32) + (f >= third_end).astype(jnp.int32)
        for f in range(3)
    ]
    hidden = []
    for f in range(3):
        row = jnp.full((1, WIDE), NEGATIVE, f32)
        for k in range(f + 1):
            seen = jnp.where(group[f] == group[k], 0.0, NEGATIVE).astype(f32)
            row = jnp.where((lane >= FRAME * k) & (lane < FRAME * (k + 1)), seen, row)
        hidden.append(row)
    frame = [((lane >= FRAME * f) & (lane < FRAME * (f + 1))).astype(f32) for f in range(3)]
    return hidden, frame


def params(**more):
    return pltpu.CompilerParams(vmem_limit_bytes=VMEM_LIMIT, **more)


def whole(*shape):
    return pl.BlockSpec(shape, lambda *_: (0,) * len(shape))


def shape_of(shape, dtype):
    return jax.ShapeDtypeStruct(shape, dtype)


def pack_early(qkv_ref, gain_ref, offset_ref, qv_ref, out_ref, rows_ref):
    rows_ref[...] = jnp.zeros_like(rows_ref)
    weight = qkv_ref[...].astype(f32)
    gain = gain_ref[...].astype(f32).reshape(1, 3)
    offset = offset_ref[...].astype(f32).reshape(1, 3)
    qv = qv_ref[...].astype(f32).reshape(1, 6)
    for r in range(3):
        for j in range(9):
            rows_ref[10 * r + j : 10 * r + j + 1, :] = weight[r : r + 1, 128 * j : 128 * j + 128]
        rows_ref[10 * r + 9 : 10 * r + 10, 0:1] = gain[:, r : r + 1]
        rows_ref[10 * r + 9 : 10 * r + 10, 1:2] = offset[:, r : r + 1]
        rows_ref[10 * r + 9 : 10 * r + 10, 2:4] = qv[:, 2 * r : 2 * r + 2]
    out_ref[...] = jnp.broadcast_to(rows_ref[...].astype(bf16)[None], out_ref.shape)


def pack_late(out_w_ref, up_ref, down_ref, out_b_ref, gain_ref, offset_ref, down_b_ref, up_b_ref, out_ref, rows_ref):
    rows_ref[...] = jnp.zeros_like(rows_ref)
    out_w = out_w_ref[...].astype(f32)
    up = up_ref[...].astype(f32)
    down = down_ref[...].astype(f32)
    vectors = [ref[...].astype(f32).reshape(1, 3) for ref in (out_b_ref, gain_ref, offset_ref, down_b_ref)]
    for r in range(3):
        for j in range(3):
            rows_ref[3 * r + j : 3 * r + j + 1, :] = out_w[r : r + 1, 128 * j : 128 * j + 128]
        for j in range(12):
            rows_ref[9 + 12 * r + j : 10 + 12 * r + j, :] = up[r : r + 1, 128 * j : 128 * j + 128]
        for k, vector in enumerate(vectors):
            rows_ref[81 + r : 82 + r, k : k + 1] = vector[:, r : r + 1]
    for r in range(12):
        for j in range(3):
            rows_ref[45 + 3 * r + j : 46 + 3 * r + j, :] = down[r : r + 1, 128 * j : 128 * j + 128]
    rows_ref[84:85, 0:12] = up_b_ref[...].astype(f32).reshape(1, 12)
    out_ref[...] = jnp.broadcast_to(rows_ref[...].astype(bf16)[None], out_ref.shape)


def run_pack_early(*args):
    return pl.pallas_call(
        pack_early,
        out_shape=shape_of((CHIPS, EARLY_ROWS, 128), bf16),
        scratch_shapes=[pltpu.VMEM((EARLY_ROWS, 128), f32)],
        compiler_params=params(),
        name="pack_early",
    )(*args)


def run_pack_late(*args):
    return pl.pallas_call(
        pack_late,
        out_shape=shape_of((CHIPS, LATE_ROWS, 128), bf16),
        scratch_shapes=[pltpu.VMEM((LATE_ROWS, 128), f32)],
        compiler_params=params(),
        name="pack_late",
    )(*args)


def total(arrived_ref):
    return jnp.sum(arrived_ref[...].astype(f32), axis=0)


def spread_lanes(rows, lane, width):
    index = lax.broadcasted_iota(jnp.int32, (1, width), 1)
    out = jnp.zeros((1, width), f32)
    for k, row in enumerate(rows):
        out = jnp.where(index == k, row[:, lane : lane + 1], out)
    return out.reshape(width)


def unpack_first(arrived_ref, qkv_ref, gain_ref, offset_ref, qv_ref):
    sums = total(arrived_ref)
    more = []
    for r in range(3):
        for j in range(9):
            qkv_ref[r : r + 1, 128 * j : 128 * j + 128] = sums[10 * r + j : 10 * r + j + 1, :]
        row = sums[10 * r + 9 : 10 * r + 10, :]
        more.append(row[:, 0:4] + row[:, 4:8])
    gain_ref[...] = spread_lanes(more, 0, 3)
    offset_ref[...] = spread_lanes(more, 1, 3)
    index = lax.broadcasted_iota(jnp.int32, (1, 6), 1)
    out = jnp.zeros((1, 6), f32)
    for k in range(6):
        out = jnp.where(index == k, more[k // 2][:, 2 + k % 2 : 3 + k % 2], out)
    qv_ref[...] = out.reshape(6)


def run_unpack_first(arrived):
    return pl.pallas_call(
        unpack_first,
        out_shape=[shape_of((3, 3 * WIDTH), f32), shape_of((3,), f32), shape_of((3,), f32), shape_of((6,), f32)],
        compiler_params=params(),
        name="unpack_first",
    )(arrived)


def unpack_rest(arrived_ref, out_ref, up_ref, down_ref, out_b_ref, gain_ref, offset_ref, down_b_ref, up_b_ref):
    sums = total(arrived_ref)
    more = []
    for r in range(3):
        for j in range(3):
            out_ref[r : r + 1, 128 * j : 128 * j + 128] = sums[3 * r + j : 3 * r + j + 1, :]
        for j in range(12):
            up_ref[r : r + 1, 128 * j : 128 * j + 128] = sums[9 + 12 * r + j : 10 + 12 * r + j, :]
        row = sums[81 + r : 82 + r, :]
        more.append(row[:, 0:4] + row[:, 4:8])
    for r in range(12):
        for j in range(3):
            down_ref[r : r + 1, 128 * j : 128 * j + 128] = sums[45 + 3 * r + j : 46 + 3 * r + j, :]
    for k, ref in enumerate((out_b_ref, gain_ref, offset_ref, down_b_ref)):
        ref[...] = spread_lanes(more, k, 3)
    up_b_ref[...] = (sums[84:85, 0:12] + sums[84:85, 12:24]).reshape(12)


def run_unpack_rest(arrived):
    return pl.pallas_call(
        unpack_rest,
        out_shape=[shape_of((3, WIDTH), f32), shape_of((3, HIDDEN), f32), shape_of((12, WIDTH), f32)]
        + [shape_of((3,), f32)] * 4
        + [shape_of((12,), f32)],
        compiler_params=params(),
        name="unpack_rest",
    )(arrived)


def attention_forward(core_ref, counts_ref, tokens_ref, own_ref, other_ref,
                      mixed_ref, query_ref, key_ref, value_ref, weight_ref, vector_ref,
                      first_ref, projected_ref, mixed_scratch, arrived_ref, bias_ref):
    slot = pl.program_id(0)
    span = tokens_ref.shape[1]
    scale = math.log2(math.e) / math.sqrt(HEAD)

    @pl.when(slot == 0)
    def _():
        core = core_ref[0]
        for side, ref in ((core, own_ref), (1 - core, other_ref)):
            blocks = jnp.swapaxes(ref[...], 0, 1)
            for r in range(3):
                at = pl.multiple_of(side * 192 + 64 * r, 64)
                for j in range(10):
                    arrived_ref[pl.ds(at, 64), 128 * j : 128 * j + 128] = blocks[10 * r + j]
        order = arrival_order()
        ordered = dot(order, arrived_ref[...], (1, 0))
        weight_ref[...] = ordered[:, : 3 * WIDTH].astype(bf16)
        vector_ref[...] = dot(arrived_ref[:, 3 * WIDTH :], order, (0, 1))[0:8]
        for s in range(2):
            column = ordered[:, 3 * WIDTH + 2 + s : 3 * WIDTH + 3 + s]
            bias_ref[pl.ds(s, WIDTH, stride=2), :] = jnp.broadcast_to(column, (WIDTH, 128))

    normed, _ = norm_parts(tokens_ref[0].astype(f32))
    first_ref[576:WIDE, :] = jnp.zeros((WIDE - 576, WIDTH), bf16)
    first_ref[0:span, :] = (normed * vector_ref[0:1] + vector_ref[1:2]).astype(bf16)
    projected_ref[...] = dot(weight_ref[...], first_ref[...], (0, 1))
    hidden, frame = mask_rows(counts_ref, slot)
    one = jnp.ones((1, WIDE), f32)
    query_more = rows_of(frame, WIDE)
    key_more = rows_of(hidden + [one, one, one], WIDE)
    value_more = rows_of([one, one, one], WIDE)

    def head_step(h, _):
        at = pl.multiple_of(h * HEAD, 8)
        to = pl.multiple_of(h * 32, 32)
        wide = lambda start: jnp.concatenate([bias_ref[pl.ds(start, HEAD), :]] * (WIDE // 128), 1)
        query = (projected_ref[pl.ds(at, HEAD), :] + wide(at)) * scale
        value = projected_ref[pl.ds(at + 2 * WIDTH, HEAD), :] + wide(at + WIDTH)
        query = jnp.concatenate([query, query_more], 0)
        key = jnp.concatenate([projected_ref[pl.ds(at + WIDTH, HEAD), :], key_more], 0).astype(bf16)
        value = jnp.concatenate([value, value_more], 0).astype(bf16)
        query_low = query.astype(bf16)
        logs = []
        for low, high, keys in FORWARD_BLOCKS:
            scores = dot(key[:, :keys], query_low[:, low:high], (0, 0))
            peak = jnp.max(scores, axis=0, keepdims=True)
            weights = jnp.exp2(scores - peak).astype(bf16)
            got = dot(value[:, :keys], weights, (1, 0))
            row_total = got[HEAD : HEAD + 1]
            mixed_scratch[pl.ds(at, HEAD), low:high] = got[:HEAD] / row_total
            logs.append(peak + jnp.log2(row_total))
        parts = three_parts(-jnp.concatenate(logs, 1))
        zero = jnp.zeros((1, WIDE), f32)
        log_rows = rows_of([zero, zero, zero, *parts], WIDE)
        query_ref[0, pl.ds(to, 32), :] = (query + jnp.concatenate([jnp.zeros((HEAD, WIDE), f32), log_rows], 0)).astype(bf16)
        key_ref[0, pl.ds(to, 32), :] = key
        value_ref[0, pl.ds(to, 32), :] = value
        return 0

    lax.fori_loop(0, HEADS, head_step, 0, unroll=2)
    mixed_ref[0] = mixed_scratch[...].astype(bf16)


def run_forward(core, counts, tokens, own, other):
    slots, span, _ = tokens.shape
    per_slot = lambda rows: pl.BlockSpec((1, rows, WIDE), lambda s: (s, 0, 0))
    scalars = pl.BlockSpec(memory_space=pltpu.SMEM)
    return pl.pallas_call(
        attention_forward,
        grid=(slots,),
        in_specs=[
            scalars,
            scalars,
            pl.BlockSpec((1, span, WIDTH), lambda s: (s, 0, 0)),
            whole(CHIPS, EARLY_ROWS, 128),
            whole(CHIPS, EARLY_ROWS, 128),
        ],
        out_specs=[per_slot(WIDTH), per_slot(512), per_slot(512), per_slot(512), whole(WIDTH, 3 * WIDTH), whole(8, WIDTH)],
        out_shape=[shape_of((slots, rows, WIDE), bf16) for rows in (WIDTH, 512, 512, 512)]
        + [shape_of((WIDTH, 3 * WIDTH), bf16), shape_of((8, WIDTH), f32)],
        scratch_shapes=[
            pltpu.VMEM((WIDE, WIDTH), bf16),
            pltpu.VMEM((3 * WIDTH, WIDE), f32),
            pltpu.VMEM((WIDTH, WIDE), f32),
            pltpu.VMEM((WIDTH, 3 * WIDTH + 128), bf16),
            pltpu.VMEM((2 * WIDTH, 128), f32),
        ],
        compiler_params=params(),
        name="attention_forward",
    )(core, counts, tokens, own, other)


def feed_forward(core_ref, tokens_ref, mixed_ref, cotangent_ref, own_ref, other_ref,
                 output_ref, grad_resid_ref, grad_mixed_ref, mine_ref, theirs_ref,
                 arrived_ref, out_w_ref, up_w_ref, down_w_ref, row_ref, up_b_ref,
                 grad_out_ref, grad_up_ref, grad_down_ref, vector_ref, up_vector_ref, packed_ref):
    slot = pl.program_id(0)
    span = tokens_ref.shape[1]
    chunk = 384

    @pl.when(slot == 0)
    def _():
        core = core_ref[0]
        for side, ref in ((core, own_ref), (1 - core, other_ref)):
            blocks = jnp.swapaxes(ref[...], 0, 1)
            for r in range(3):
                at = pl.multiple_of(side * 192 + 64 * r, 64)
                for j in range(15):
                    arrived_ref[pl.ds(at, 64), 128 * j : 128 * j + 128] = blocks[3 * r + j] if j < 3 else blocks[6 + 12 * r + j]
                arrived_ref[pl.ds(at, 64), 1920:2048] = blocks[81 + r]
            for r in range(12):
                at = pl.multiple_of(side * 768 + 64 * r, 64)
                for j in range(3):
                    down_w_ref[pl.ds(at, 64), 128 * j : 128 * j + 128] = blocks[45 + 3 * r + j]
            turned = blocks[84].astype(f32).T
            up_b = jnp.concatenate([turned[r : r + 1] for r in range(12)], 1)
            up_b_ref[:, pl.ds(pl.multiple_of(side * 768, 128), 768)] = up_b
        order = arrival_order()
        ordered = dot(order, arrived_ref[:, :1920], (1, 0)).astype(bf16)
        out_w_ref[...] = ordered[:, :WIDTH]
        up_w_ref[...] = ordered[:, WIDTH:]
        row_ref[...] = dot(arrived_ref[:, 1920:], order, (0, 1))[0:8]
        grad_out_ref[...] = jnp.zeros_like(grad_out_ref)
        grad_up_ref[...] = jnp.zeros_like(grad_up_ref)
        grad_down_ref[...] = jnp.zeros_like(grad_down_ref)
        vector_ref[...] = jnp.zeros_like(vector_ref)
        up_vector_ref[...] = jnp.zeros_like(up_vector_ref)

    out_b, gain, offset, down_b = (row_ref[k : k + 1] for k in range(4))
    mixed = mixed_ref[0]
    mixed = mixed[:, :span]
    resid = tokens_ref[0].astype(f32) + dot(mixed, out_w_ref[...], (0, 0)) + out_b
    normed, inverse = norm_parts(resid)
    second = (normed * gain + offset).astype(bf16)
    grad_branch = cotangent_ref[0]
    result = resid + down_b
    grad_second = jnp.zeros((span, WIDTH), f32)
    root = math.sqrt(2.0 / math.pi)
    for at in range(0, HIDDEN, chunk):
        cols = slice(at, at + chunk)
        up = dot(second, up_w_ref[:, cols], (1, 0)) + up_b_ref[:, cols]
        square = up * up
        tanh = jnp.tanh(up * (root + (root * 0.044715) * square))
        half = 0.5 + 0.5 * tanh
        activated = (up * half).astype(bf16)
        slope = half + (up * (2.0 * half * (1.0 - half))) * (root + (3 * root * 0.044715) * square)
        result += dot(activated, down_w_ref[cols, :], (1, 0))
        grad_up = (dot(grad_branch, down_w_ref[cols, :], (1, 1)) * slope).astype(bf16)
        grad_down_ref[cols, :] += dot(activated, grad_branch, (0, 0))
        grad_up_ref[:, cols] += dot(second, grad_up, (0, 0))
        up_vector_ref[:, cols] += jnp.sum(grad_up.astype(f32), axis=0, keepdims=True)
        grad_second += dot(grad_up, up_w_ref[:, cols], (1, 1))
    output_ref[0] = result.astype(bf16)
    scaled = grad_second * gain
    mean_one = jnp.mean(scaled, axis=-1, keepdims=True)
    mean_two = jnp.mean(scaled * normed, axis=-1, keepdims=True)
    grad_full = grad_branch.astype(f32)
    grad_resid = grad_full + inverse * (scaled - mean_one - normed * mean_two)
    grad_resid_ref[0] = grad_resid
    attended = grad_resid.astype(bf16)
    grad_out_ref[...] += dot(mixed, attended, (1, 0))
    grad_mixed_ref[0] = jnp.zeros_like(grad_mixed_ref[0])
    grad_mixed_ref[0, :, :span] = dot(out_w_ref[...], attended, (1, 1)).astype(bf16)
    vector_ref[0:1] += jnp.sum(attended.astype(f32), axis=0, keepdims=True)
    vector_ref[1:2] += jnp.sum(grad_second * normed, axis=0, keepdims=True)
    vector_ref[2:3] += jnp.sum(grad_second, axis=0, keepdims=True)
    vector_ref[3:4] += jnp.sum(grad_full, axis=0, keepdims=True)

    @pl.when(slot == pl.num_programs(0) - 1)
    def _():
        core = core_ref[0]
        order = arrival_order()
        packed_ref[:, :WIDTH] = dot(order, grad_out_ref[...].astype(bf16), (0, 0)).astype(bf16)
        packed_ref[:, WIDTH:1920] = dot(order, grad_up_ref[...].astype(bf16), (0, 0)).astype(bf16)
        high, low = two_parts(vector_ref[0:4])
        rows = jnp.concatenate([high, low, jnp.zeros((120, WIDTH), f32)], 0).astype(bf16)
        packed_ref[:, 1920:] = dot(order, rows, (0, 1)).astype(bf16)
        blank = jnp.zeros((CHIPS, 128), bf16)
        for side, ref in ((core, mine_ref), (1 - core, theirs_ref)):
            blocks = [blank] * LATE_ROWS
            for r in range(3):
                at = pl.multiple_of(side * 192 + 64 * r, 64)
                for j in range(15):
                    blocks[3 * r + j if j < 3 else 6 + 12 * r + j] = packed_ref[pl.ds(at, 64), 128 * j : 128 * j + 128]
                blocks[81 + r] = packed_ref[pl.ds(at, 64), 1920:2048]
            for r in range(12):
                at = pl.multiple_of(side * 768 + 64 * r, 64)
                for j in range(3):
                    blocks[45 + 3 * r + j] = grad_down_ref[pl.ds(at, 64), 128 * j : 128 * j + 128].astype(bf16)
            line = up_vector_ref[:, pl.ds(pl.multiple_of(side * 768, 128), 768)]
            high, low = two_parts(line)
            rows = [part[:, 64 * r : 64 * r + 64] for part in (high, low) for r in range(12)]
            blocks[84] = rows_of(rows, 64, 128).T.astype(bf16)
            ref[...] = jnp.swapaxes(jnp.stack(blocks), 0, 1)


def run_feed_forward(core, tokens, mixed, cotangent, own, other):
    slots, span, _ = tokens.shape
    rows = pl.BlockSpec((1, span, WIDTH), lambda s: (s, 0, 0))
    turned = pl.BlockSpec((1, WIDTH, WIDE), lambda s: (s, 0, 0))
    message = whole(CHIPS, LATE_ROWS, 128)
    return pl.pallas_call(
        feed_forward,
        grid=(slots,),
        in_specs=[pl.BlockSpec(memory_space=pltpu.SMEM), rows, turned, rows, message, message],
        out_specs=[rows, rows, turned, message, message],
        out_shape=[
            shape_of((slots, span, WIDTH), bf16),
            shape_of((slots, span, WIDTH), f32),
            shape_of((slots, WIDTH, WIDE), bf16),
            shape_of((CHIPS, LATE_ROWS, 128), bf16),
            shape_of((CHIPS, LATE_ROWS, 128), bf16),
        ],
        scratch_shapes=[
            pltpu.VMEM((WIDTH, 2048), bf16),
            pltpu.VMEM((WIDTH, WIDTH), bf16),
            pltpu.VMEM((WIDTH, HIDDEN), bf16),
            pltpu.VMEM((HIDDEN, WIDTH), bf16),
            pltpu.VMEM((8, WIDTH), f32),
            pltpu.VMEM((1, HIDDEN), f32),
            pltpu.VMEM((WIDTH, WIDTH), f32),
            pltpu.VMEM((WIDTH, HIDDEN), f32),
            pltpu.VMEM((HIDDEN, WIDTH), f32),
            pltpu.VMEM((8, WIDTH), f32),
            pltpu.VMEM((1, HIDDEN), f32),
            pltpu.VMEM((WIDTH, 2048), bf16),
        ],
        compiler_params=params(),
        name="feed_forward",
    )(core, tokens, mixed, cotangent, own, other)


def attention_backward(core_ref, tokens_ref, query_ref, key_ref, value_ref, mixed_ref, grad_mixed_ref, grad_resid_ref, weight_ref, row_ref,
                       input_grad_ref, mine_ref, theirs_ref,
                       first_ref, turned_ref, grad_weight_ref, grad_bias_ref, vector_ref, packed_ref):
    slot = pl.program_id(0)
    span = tokens_ref.shape[1]

    @pl.when(slot == 0)
    def _():
        grad_weight_ref[...] = jnp.zeros_like(grad_weight_ref)
        grad_bias_ref[...] = jnp.zeros_like(grad_bias_ref)
        vector_ref[...] = jnp.zeros_like(vector_ref)

    gain, offset = row_ref[0:1], row_ref[1:2]
    normed, inverse = norm_parts(tokens_ref[0].astype(f32))
    first_ref[576:WIDE, :] = jnp.zeros((WIDE - 576, WIDTH), bf16)
    first_ref[0:span, :] = (normed * gain + offset).astype(bf16)

    def head_step(pair, _):
        for part in range(2):
            h = pair * 2 + part
            to = pl.multiple_of(h * 32, 32)
            at = pl.multiple_of(h * HEAD, 8)
            query = query_ref[0, pl.ds(to, 32), :]
            key = key_ref[0, pl.ds(to, 32), :]
            value = value_ref[0, pl.ds(to, 32), :]
            both = pl.multiple_of(pair * 48, 16)
            grad = grad_mixed_ref[0, pl.ds(both, 48), :].astype(f32)[HEAD * part : HEAD * part + HEAD]
            mixed = mixed_ref[0, pl.ds(both, 48), :].astype(f32)[HEAD * part : HEAD * part + HEAD]
            shift = jnp.sum(grad * mixed, axis=0, keepdims=True)
            grad = jnp.concatenate([grad, rows_of(three_parts(-shift), WIDE)], 0).astype(bf16)
            grad_q = []
            grad_k = jnp.zeros((32, WIDE), f32)
            grad_v = jnp.zeros((32, WIDE), f32)
            for low, high, keys in BACKWARD_BLOCKS:
                probs = jnp.exp2(dot(query[:, low:high], key[:, :keys], (0, 0)))
                grad_scores = (probs * dot(grad[:, low:high], value[:, :keys], (0, 0))).astype(bf16)
                probs_low = probs.astype(bf16)
                more_v = dot(grad[:, low:high], probs_low, (1, 0))
                more_k = dot(query[:, low:high], grad_scores, (1, 0))
                grad_q.append(dot(key[:, :keys], grad_scores, (1, 1)))
                if keys < WIDE:
                    blank = jnp.zeros((32, WIDE - keys), f32)
                    more_v = jnp.concatenate([more_v, blank], 1)
                    more_k = jnp.concatenate([more_k, blank], 1)
                grad_v += more_v
                grad_k += more_k
            grad_q.append(jnp.zeros((32, WIDE - 592), f32))
            grad_q = jnp.concatenate(grad_q, 1)
            turned_ref[pl.ds(at, HEAD), :] = grad_q[:HEAD] * (1.0 / math.sqrt(HEAD))
            turned_ref[pl.ds(at + WIDTH, HEAD), :] = grad_k[:HEAD] * math.log(2.0)
            turned_ref[pl.ds(at + 2 * WIDTH, HEAD), :] = grad_v[:HEAD]
        return 0

    lax.fori_loop(0, HEADS // 2, head_step, 0)
    turned = turned_ref[...].astype(bf16)
    sums = jnp.sum(turned.astype(f32), axis=1, keepdims=True)
    grad_bias_ref[0:WIDTH] += jnp.broadcast_to(sums[:WIDTH], (WIDTH, 128))
    grad_bias_ref[WIDTH:] += jnp.broadcast_to(sums[2 * WIDTH :], (WIDTH, 128))
    grad_weight_ref[...] += dot(first_ref[...], turned, (0, 1))
    grad_first = dot(turned, weight_ref[...], (0, 1))[:span]
    scaled = grad_first * gain
    mean_one = jnp.mean(scaled, axis=-1, keepdims=True)
    mean_two = jnp.mean(scaled * normed, axis=-1, keepdims=True)
    input_grad_ref[0] = grad_resid_ref[0] + inverse * (scaled - mean_one - normed * mean_two)
    vector_ref[0:1] += jnp.sum(grad_first * normed, axis=0, keepdims=True)
    vector_ref[1:2] += jnp.sum(grad_first, axis=0, keepdims=True)

    @pl.when(slot == pl.num_programs(0) - 1)
    def _():
        core = core_ref[0]
        order = arrival_order()
        packed_ref[:, : 3 * WIDTH] = dot(order, grad_weight_ref[...].astype(bf16), (0, 0)).astype(bf16)
        blank = jnp.zeros((2, WIDTH), f32)
        high, low = two_parts(vector_ref[0:2])
        rows = jnp.concatenate([high, blank, low, jnp.zeros((122, WIDTH), f32)], 0).astype(bf16)
        more = dot(order, rows, (0, 1))
        lane = lax.broadcasted_iota(jnp.int32, (WIDTH, 128), 1)
        columns = jnp.zeros((WIDTH, 128), f32)
        for s in range(2):
            high, low = two_parts(grad_bias_ref[pl.ds(s, WIDTH, stride=2), :])
            columns = jnp.where(lane == 2 + s, high, jnp.where(lane == 6 + s, low, columns))
        more += dot(order, columns.astype(bf16), (0, 0))
        packed_ref[:, 3 * WIDTH :] = more.astype(bf16)
        blank = jnp.zeros((CHIPS, 128), bf16)
        for side, ref in ((core, mine_ref), (1 - core, theirs_ref)):
            blocks = []
            for r in range(3):
                at = pl.multiple_of(side * 192 + 64 * r, 64)
                for j in range(10):
                    blocks.append(packed_ref[pl.ds(at, 64), 128 * j : 128 * j + 128])
            ref[...] = jnp.swapaxes(jnp.stack(blocks + [blank, blank]), 0, 1)


def run_backward(core, tokens, query, key, value, mixed, grad_mixed, grad_resid, weight, row):
    slots, span, _ = tokens.shape
    rows = pl.BlockSpec((1, span, WIDTH), lambda s: (s, 0, 0))
    turned = lambda n: pl.BlockSpec((1, n, WIDE), lambda s: (s, 0, 0))
    message = whole(CHIPS, EARLY_ROWS, 128)
    return pl.pallas_call(
        attention_backward,
        grid=(slots,),
        in_specs=[pl.BlockSpec(memory_space=pltpu.SMEM), rows, turned(512), turned(512), turned(512), turned(WIDTH), turned(WIDTH), rows,
                  whole(WIDTH, 3 * WIDTH), whole(8, WIDTH)],
        out_specs=[rows, message, message],
        out_shape=[
            shape_of((slots, span, WIDTH), f32),
            shape_of((CHIPS, EARLY_ROWS, 128), bf16),
            shape_of((CHIPS, EARLY_ROWS, 128), bf16),
        ],
        scratch_shapes=[
            pltpu.VMEM((WIDE, WIDTH), bf16),
            pltpu.VMEM((3 * WIDTH, WIDE), f32),
            pltpu.VMEM((WIDTH, 3 * WIDTH), f32),
            pltpu.VMEM((2 * WIDTH, 128), f32),
            pltpu.VMEM((8, WIDTH), f32),
            pltpu.VMEM((WIDTH, 3 * WIDTH + 128), bf16),
        ],
        compiler_params=params(),
        name="attention_backward",
    )(core, tokens, query, key, value, mixed, grad_mixed, grad_resid, weight, row)


def to_chips(message):
    return lax.all_to_all(message, CHIP_AXES, 0, 0, tiled=True)


def across(message):
    return lax.ppermute(message, CORE_AXIS, [(0, 1), (1, 0)])


def shards(tokens, item_frames, ln1_gain, ln1_bias, qkv_weight, qv_bias, out_weight, out_bias, ln2_gain, ln2_bias,
           up_weight, up_bias, down_weight, down_bias, cotangent):
    core = lax.axis_index(CORE_AXIS).astype(jnp.int32).reshape(1)
    early = to_chips(run_pack_early(qkv_weight, ln1_gain, ln1_bias, qv_bias))
    up_sent = up_weight.reshape(3, 16, 2, 4, 12).transpose(0, 2, 4, 1, 3).reshape(3, HIDDEN)
    late = to_chips(run_pack_late(out_weight, up_sent, down_weight, out_bias, ln2_gain, ln2_bias, down_bias, up_bias))
    mixed, query, key, value, weight, row = run_forward(core, item_frames, tokens, early, across(early))
    output, grad_resid, grad_mixed, mine, theirs = run_feed_forward(core, tokens, mixed, cotangent, late, across(late))
    rest = (mine.astype(f32) + across(theirs).astype(f32)).astype(bf16)
    rest = to_chips(rest)
    input_grad, mine, theirs = run_backward(core, tokens, query, key, value, mixed, grad_mixed, grad_resid, weight, row)
    own = (mine.astype(f32) + across(theirs).astype(f32)).astype(bf16)
    own = to_chips(own)
    grad_out, grad_up, grad_down, grad_out_b, grad_gain_two, grad_offset_two, grad_down_b, grad_up_b = run_unpack_rest(rest)
    grad_up = grad_up.reshape(3, 2, 12, 16, 4).transpose(0, 3, 1, 4, 2).reshape(3, HIDDEN)
    grad_qkv, grad_gain, grad_offset, grad_qv = run_unpack_first(own)
    return (output, input_grad, grad_gain, grad_offset, grad_qkv, grad_qv, grad_out, grad_out_b, grad_gain_two, grad_offset_two,
            grad_up, grad_up_b, grad_down, grad_down_b)


def solution(mesh):
    split = Mesh(mesh.devices.reshape(4, 4, 2, mesh.shape["narrow"]), ALL)
    by_rank = lambda n: P(ALL, *([None] * (n - 1)))
    return jax.shard_map(
        shards,
        mesh=split,
        in_specs=tuple(by_rank(n) for n in (3, 2, 1, 1, 2, 1, 2, 1, 1, 1, 2, 1, 2, 1, 3)),
        out_specs=tuple(by_rank(n) for n in (3, 3, 1, 1, 2, 1, 2, 1, 1, 1, 2, 1, 2, 1)),
        check_vma=False,
    )
```

time: 352 us -> 240 us (0.68)
  waiting for transfers between devices: 119 us -> 25.9 us
  blocking collectives: 0 us -> 53.2 us
  local copies, waits for them, and re-layouts: 57.5 us -> 16.3 us
  Pallas kernels: 107 us -> 124 us
  other arithmetic: 21.6 us -> 4.96 us
  starting transfers between devices: 28.3 us -> 12.4 us
  between operations: 14.2 us -> 0.76 us
    all_gather x2 -> x0, waiting for transfers between devices: 53.3 us -> none  [the longest x1 53.3 us: shards(): lax.all_gather(jnp.concatenate([out_weight, up_weight, column(out_bias),...]
    all_to_all x0 -> x2, blocking collectives: none -> 53.2 us  [to_chips(): return lax.all_to_all(message, CHIP_AXES, 0, 0, tiled=True)]
    all_to_all x4 -> x2, waiting for transfers between devices: 66.1 us -> 23.9 us  [to_chips(): return lax.all_to_all(message, CHIP_AXES, 0, 0, tiled=True)]
    concatenate x21 -> x0, local copies, waits for them, and re-layouts: 20.1 us -> none  [the longest x12 17.1 us: spread(): both = jnp.concatenate(parts, 1).astype(bf16)]
    all_to_all x4 -> x2, starting transfers between devices: 28.2 us -> 11.8 us  [to_chips(): return lax.all_to_all(message, CHIP_AXES, 0, 0, tiled=True)]
    pallas_call x3 -> x7, Pallas kernels: 107 us -> 124 us  [the longest x1 44.9 us: run_backward(): pl.pallas_call(attention_backward, grid=(slots,), in_specs=[pl.BlockSpec(...]
    another operation x6 -> x0, other arithmetic: 10.2 us -> none
    slice x14 -> x0, local copies, waits for them, and re-layouts: 8.8 us -> none  [the longest x2 1.85 us: shards(): out_w, up_w = (wide[:, :width], wide[:, width:width + hidden])]
  transfers between devices with their start and end apart: 6 -> 6, of which waited for: 5 -> 3; matrix products, arithmetic and copies ran while one was open for 15% -> 5% of each run, Pallas kernels for 11% -> 38%
where the time goes in v2:
time: 240 us; the launch traced here: 237 us
  Pallas kernels  124 us (52%)
  blocking collectives  53.2 us (22%)
  waiting for transfers between devices  25.9 us (11%)
  local copies, waits for them, and re-layouts  16.3 us (7%)
  starting transfers between devices  12.4 us (5%)
  other arithmetic  4.96 us (2%)
    all_to_all x2, blocking collectives, to_chips(): return lax.all_to_all(message, CHIP_AXES, 0, 0, tiled=True)  53.2 us
    pallas_call x1, Pallas kernels, run_backward(): pl.pallas_call(attention_backward, grid=(slots,), in_specs=[pl.BlockSpec(...  44.9 us
    pallas_call x1, Pallas kernels, run_forward(): pl.pallas_call(attention_forward, grid=(slots,), in_specs=[scalars, scala...  40.5 us
    pallas_call x1, Pallas kernels, run_feed_forward(): pl.pallas_call(feed_forward, grid=(slots,), in_specs=[pl.BlockSpec(memory...  30.3 us
    all_to_all x2, waiting for transfers between devices, to_chips(): return lax.all_to_all(message, CHIP_AXES, 0, 0, tiled=True)  23.9 us
    all_to_all x2, starting transfers between devices, to_chips(): return lax.all_to_all(message, CHIP_AXES, 0, 0, tiled=True)  11.8 us
    unnamed x22, local copies, waits for them, and re-layouts  10.8 us
  transfers between devices with their start and end apart: 6, of which 3 were waited for; matrix products, arithmetic and copies ran while one was open for 5% of the time, Pallas kernels for 38%

profile of v2, /device:TPU:2, one launch (start us, length us, event | category | flops | bytes accessed | tf_op | source)
XLA Modules:
  0.0 237.2 jit_solution(12103452068655888908)
XLA Ops:
  0.6 0.9 reshape.44
  1.6 0.7 copy.38
  2.3 1.0 reshape.45.up_ref
  3.4 2.1 pack_late.1
  5.4 34.1 %all_to_all.20.own_ref = bf16[64,96,128]{2,1,0:T(8,128)(2,1)S(1)} all-to-all(bf16[64,96,128]{2,1,0:T(8,128)(2,1)} %pack_late.1), channel_id=1, replica_groups=mesh['wide_0'=4,'wide_1'=4,'wide_2'=2,'narrow'=4] {'wide_0','wide_1','na..., dimensions={0} | all-to-all | bytes 3145728 | tf_op jit(solution)/shard_map/all_to_all | solution.py:582
  39.6 1.9 pack_early.1
  41.4 19.0 %all_to_all.21.own_ref = bf16[64,32,128]{2,1,0:T(8,128)(2,1)S(1)} all-to-all(bf16[64,32,128]{2,1,0:T(8,128)(2,1)} %pack_early.1), channel_id=1, replica_groups=mesh['wide_0'=4,'wide_1'=4,'wide_2'=2,'narrow'=4] {'wide_0','wide_1','na..., dimensions={0} | all-to-all | bytes 1048576 | tf_op jit(solution)/shard_map/all_to_all | solution.py:582
  60.5 1.0 copy.39.tokens_ref
  61.5 0.6 copy-done.7
  62.2 1.0 copy.40.cotangent_ref
  63.2 0.8 copy-done.8
  64.0 40.5 %attention_forward.1 = (bf16[2,384,640]{2,1,0:T(8,128)(2,1)}, bf16[2,512,640]{2,1,0:T(8,128)(2,1)}, bf16[2,512,640]{2,1,0:T(8,128)(2,1)}, bf16[2,512,640]{2,1,0:...) custom-call(s32[1]{0:T(128)} %bitcast.core_ref, s32[2,3]{1,0:T(2,128)} %counts_ref.1, ...), custom_call_target="tpu_custom_call" | custom-call | tf_op jit(solution)/shard_map/attention_forward/pallas_call | solution.py:294
  104.5 30.3 %feed_forward.1 = (bf16[2,588,384]{2,1,0:T(8,128)(2,1)}, f32[2,588,384]{2,1,0:T(8,128)}, bf16[2,384,640]{2,1,0:T(8,128)(2,1)}, bf16[64,96,128]{2,1,0:T(8,128)(2,1)}, bf16[64,96,128]{2,1,0:T(8,128)(2,1)}) custom-call(s32[1]{0:T(128)} %bitcast.core_ref, bf16[2,588,384]{2,1,0:T(8,128)(2,1)} %copy.39.tokens_ref, ...), custom_call_target="tpu_custom_call" | custom-call | tf_op jit(solution)/shard_map/feed_forward/pallas_call | solution.py:428
  134.8 0.4 collective-permute-start.3
  135.2 44.9 %attention_backward.1 = (f32[2,588,384]{2,1,0:T(8,128)}, bf16[64,32,128]{2,1,0:T(8,128)(2,1)}, bf16[64,32,128]{2,1,0:T(8,128)(2,1)}) custom-call(s32[1]{0:T(128)} %bitcast.core_ref, bf16[2,588,384]{2,1,0:T(8,128)(2,1)} %copy.39.tokens_ref, bf16[2,512,640]{2,1,0:T(8,128)(2,1)} %get-tuple-element.42.query_ref, bf16[2,512,640]{2,1,0:T(8,128)(2,1)} %get-tuple-element.43.key_ref, ...), custom_call_target="tpu_custom_call" | custom-call | tf_op jit(solution)/shard_map/attention_backward/pallas_call | solution.py:557
  180.1 0.2 collective-permute-start.2
  180.3 2.0 collective-permute-done.2
  182.3 2.0 add_convert_fusion.1
  184.3 5.9 %all-to-all-start.2 = ((bf16[64,32,128]{2,1,0:T(8,128)(2,1)}), bf16[64,32,128]{2,1,0:T(8,128)(2,1)S(1)}, u32[]{:S(2)}, u32[]{:S(2)}) async-start(bf16[64,32,128]{2,1,0:T(8,128)(2,1)} %add_convert_fusion.1), calls=%async_computation.2 | async-start | bytes 1048576 | tf_op jit(solution)/shard_map/all_to_all | solution.py:582
  190.2 3.0 %add_convert_fusion = bf16[64,96,128]{2,1,0:T(8,128)(2,1)} fusion(bf16[64,96,128]{2,1,0:T(8,128)(2,1)} %collective-permute-done.3, bf16[64,96,128]{2,1,0:T(8,128)(2,1)S(1)} %copy-done.4), kind=kLoop, calls=%fused_computation | loop fusion | flops 3145728 | bytes 4718592 | tf_op jit(solution)/shard_map/convert_element_type | solution.py:597
  193.2 9.4 %all-to-all-done.2.arrived_ref = bf16[64,32,128]{2,1,0:T(8,128)(2,1)S(1)} async-done(((bf16[64,32,128]{2,1,0:T(8,128)(2,1)}), bf16[64,32,128]{2,1,0:T(8,128)(2,1)S(1)}, u32[]{:S(2)}, u32[]{:S(2)}) %all-to-all-start.2) | async-done | bytes 524320 | tf_op jit(solution)/shard_map/all_to_all | solution.py:582
  202.6 0.8 copy-done.2
  203.4 5.9 %all-to-all-start.3 = ((bf16[64,96,128]{2,1,0:T(8,128)(2,1)}), bf16[64,96,128]{2,1,0:T(8,128)(2,1)S(1)}, u32[]{:S(2)}, u32[]{:S(2)}) async-start(bf16[64,96,128]{2,1,0:T(8,128)(2,1)} %add_convert_fusion), calls=%async_computation.3 | async-start | bytes 3145728 | tf_op jit(solution)/shard_map/all_to_all | solution.py:582
  209.3 1.6 copy.43
  210.9 3.6 %copy.44 = f32[2,588,384]{2,0,1:T(2,128)} copy(f32[2,588,384]{2,1,0:T(8,128)} %get-tuple-element.81) | data formatting | bytes 3612672
  214.5 1.8 unpack_first.1
  216.3 14.5 %all-to-all-done.3.arrived_ref = bf16[64,96,128]{2,1,0:T(8,128)(2,1)S(1)} async-done(((bf16[64,96,128]{2,1,0:T(8,128)(2,1)}), bf16[64,96,128]{2,1,0:T(8,128)(2,1)S(1)}, u32[]{:S(2)}, u32[]{:S(2)}) %all-to-all-start.3) | async-done | bytes 1572896 | tf_op jit(solution)/shard_map/all_to_all | solution.py:582
  230.8 1.2 copy-done
  232.0 2.3 unpack_rest.1
  234.3 1.3 reshape.46
  235.7 0.7 copy.42
  236.4 0.8 reshape.47
  (19 shorter events, 0.0 us)
Async XLA Ops:
  39.6 22.0 %copy-start.1 = (bf16[64,96,128]{2,1,0:T(8,128)(2,1)}, bf16[64,96,128]{2,1,0:T(8,128)(2,1)S(1)}, u32[]{:S(2)}) copy-start(bf16[64,96,128]{2,1,0:T(8,128)(2,1)S(1)} %all_to_all.20.own_ref) | copy-start | bytes 4718596
  39.6 20.9 %copy-start.6 = (bf16[2,588,384]{2,0,1:T(2,128)(2,1)S(1)}, bf16[2,588,384]{2,0,1:T(2,128)(2,1)}, u32[]{:S(2)}) copy-start(bf16[2,588,384]{2,0,1:T(2,128)(2,1)} %param.15) | copy-start | bytes 2709508
  39.6 64.9 %collective-permute-start.1 = (bf16[64,96,128]{2,1,0:T(8,128)(2,1)S(1)}, bf16[64,96,128]{2,1,0:T(8,128)(2,1)}, u32[]{:S(2)}, u32[]{:S(2)}) collective-permute-start(bf16[64,96,128]{2,1,0:T(8,128)(2,1)S(1)} %all_to_all.20.own_ref), channel_id=1, source_target_pairs={{0,4},{4,0},{1,5},{5,1},{2,6},{6,2},{3,7},{7,3},{8,12},{12,8},{9,1... | collective-permute-start | bytes 4718600 | tf_op jit(solution)/shard_map/ppermute | solution.py:586
  60.5 2.8 %copy-start.3 = (bf16[64,32,128]{2,1,0:T(8,128)(2,1)}, bf16[64,32,128]{2,1,0:T(8,128)(2,1)S(1)}, u32[]{:S(2)}) copy-start(bf16[64,32,128]{2,1,0:T(8,128)(2,1)S(1)} %all_to_all.21.own_ref) | copy-start | bytes 1572868
  60.5 2.8 %collective-permute-start = (bf16[64,32,128]{2,1,0:T(8,128)(2,1)S(1)}, bf16[64,32,128]{2,1,0:T(8,128)(2,1)S(1)}, u32[]{:S(2)}, u32[]{:S(2)}) collective-permute-start(bf16[64,32,128]{2,1,0:T(8,128)(2,1)S(1)} %all_to_all.21.own_ref), channel_id=1, source_target_pairs={{0,4},{4,0},{1,5},{5,1},{2,6},{6,2},{3,7},{7,3},{8,12},{12,8},{9,1... | collective-permute-start | bytes 1572872 | tf_op jit(solution)/shard_map/ppermute | solution.py:586
  60.5 1.7 copy-start.7
  63.2 0.8 copy-start.8
  134.8 55.3 %collective-permute-start.3 = (bf16[64,96,128]{2,1,0:T(8,128)(2,1)}, bf16[64,96,128]{2,1,0:T(8,128)(2,1)}, u32[]{:S(2)}, u32[]{:S(2)}) collective-permute-start(bf16[64,96,128]{2,1,0:T(8,128)(2,1)} %get-tuple-element.57), channel_id=1, source_target_pairs={{0,4},{4,0},{1,5},{5,1},{2,6},{6,2},{3,7},{7,3},{8,12},{12,8},{9,1... | collective-permute-start | bytes 4718600 | tf_op jit(solution)/shard_map/ppermute | solution.py:586
  180.1 10.1 %copy-start.4 = (bf16[64,96,128]{2,1,0:T(8,128)(2,1)S(1)}, bf16[64,96,128]{2,1,0:T(8,128)(2,1)}, u32[]{:S(2)}) copy-start(bf16[64,96,128]{2,1,0:T(8,128)(2,1)} %get-tuple-element.56) | copy-start | bytes 4718596
  180.1 2.2 collective-permute-start.2
  184.3 18.3 %all-to-all-start.2 = ((bf16[64,32,128]{2,1,0:T(8,128)(2,1)}), bf16[64,32,128]{2,1,0:T(8,128)(2,1)S(1)}, u32[]{:S(2)}, u32[]{:S(2)}) async-start(bf16[64,32,128]{2,1,0:T(8,128)(2,1)} %add_convert_fusion.1), calls=%async_computation.2 | async-start | bytes 1048576 | tf_op jit(solution)/shard_map/all_to_all | solution.py:582
  193.2 16.1 %copy-start.5 = (bf16[2,588,384]{2,1,0:T(8,128)(2,1)S(1)}, bf16[2,588,384]{2,1,0:T(8,128)(2,1)}, u32[]{:S(2)}) copy-start(bf16[2,588,384]{2,1,0:T(8,128)(2,1)} %get-tuple-element.80) | copy-start | bytes 2709508
  202.6 0.8 copy-start.2
  203.4 27.5 %all-to-all-start.3 = ((bf16[64,96,128]{2,1,0:T(8,128)(2,1)}), bf16[64,96,128]{2,1,0:T(8,128)(2,1)S(1)}, u32[]{:S(2)}, u32[]{:S(2)}) async-start(bf16[64,96,128]{2,1,0:T(8,128)(2,1)} %add_convert_fusion), calls=%async_computation.3 | async-start | bytes 3145728 | tf_op jit(solution)/shard_map/all_to_all | solution.py:582
  230.8 1.2 copy-start
